TPU v7x, 128 devices: a whole 4x4x4 slice. The times are simulated.
128 devices in a mesh: row: 4 (over z), bulk: 32 (over y, x, core).
Axes of the slice: x: 4, y: 4, z: 4, core: 2. Of those that a mesh axis runs over, the one named last changes fastest.
Arguments:
- density: bfloat16 [96, 96, 128, 128], P('row', 'bulk'), may hold values from -6 to 6
- factors: bfloat16 [96, 384, 128], replicated, may hold values from -0.5 to 0.5
- core: float32 [384, 384], replicated, as said below
- task_blocks: int32 [128, 12], P(('row', 'bulk')), may hold values from 0 to 95, as said below
- quartets: int32 [16384, 4], P(('row', 'bulk')), may hold values from 0 to 11
- quartet_count: int32 [128], P(('row', 'bulk')), may hold values from 1 to 128, as said below
Outputs:
- fock: float32 [96, 96, 128, 128], P('row', 'bulk')
Inputs may be any that keep to these rules, and one draw needn't show every extreme that they name: `task_blocks`: each row holds 12 distinct shell blocks: entries g * 3 to g * 3 + 2 lie in blocks g * 24 to g * 24 + 23, and no two entries of a row lie in the same aligned group of 3 blocks. `quartet_count`: some device has all 128 slots live, and another one has a single live slot. core[p, q] = core[q, p].
All inputs are finite; a program needn't handle non-finite values.
Results may differ from a plain program's by a relative error of at most 0.015.
Values may be sent and summed in bfloat16 or wider, within the bound.
A program may use at most 256 MiB of HBM per device.

v0:
```python
import jax
import jax.numpy as jnp
from jax import lax
from jax.sharding import PartitionSpec as P


def pair_table(targets, sources, weights, npairs):
    labels = jnp.arange(npairs, dtype=jnp.int32)
    hot_target = (targets[:, None] == labels[None, :]).astype(jnp.float32)
    hot_source = (sources[:, None] == labels[None, :]).astype(jnp.float32) * weights[:, None]
    return jnp.einsum("ut,us->ts", hot_target, hot_source, precision=lax.Precision.HIGHEST)


def shards(density, factors, core, task_blocks, quartets, quartet_count):
    rows_axis = lax.axis_size("row")
    bulk_axis = lax.axis_size("bulk")
    devices = rows_axis * bulk_axis
    blocks = task_blocks[0]
    count = quartet_count[0]
    ntask = blocks.shape[0]
    npairs = ntask * ntask
    slots = ntask // rows_axis
    row_blocks = density.shape[0]
    col_blocks = density.shape[1]
    width = density.shape[2]
    points = factors.shape[1]
    my_row = lax.axis_index("row")
    my_bulk = lax.axis_index("bulk")
    positions = jnp.arange(ntask, dtype=jnp.int32)
    left_ids = jnp.broadcast_to(blocks[:, None], (ntask, ntask))
    right_ids = jnp.broadcast_to(blocks[None, :], (ntask, ntask))
    target = left_ids // row_blocks * bulk_axis + right_ids // col_blocks
    slot_of = jnp.broadcast_to((positions % slots)[:, None], (ntask, ntask))
    pair_ids = jnp.stack([left_ids, right_ids], axis=-1).reshape(-1, 2)
    requests = jnp.full((devices, slots, 2), -1, jnp.int32)
    requests = requests.at[target.reshape(-1), slot_of.reshape(-1)].set(pair_ids)

    def local_place(incoming):
        valid = incoming[..., 0] >= 0
        local_row = jnp.clip(incoming[..., 0] - my_row * row_blocks, 0, row_blocks - 1)
        local_col = jnp.clip(incoming[..., 1] - my_bulk * col_blocks, 0, col_blocks - 1)
        return (valid, local_row, local_col)

    incoming = lax.all_to_all(requests, ("row", "bulk"), split_axis=0, concat_axis=0, tiled=True)
    valid, local_row, local_col = local_place(incoming)
    found = density[local_row, local_col]
    replies = lax.all_to_all(
        jnp.where(valid[:, :, None, None], found, jnp.zeros_like(found)),
        ("row", "bulk"),
        split_axis=0,
        concat_axis=0,
        tiled=True,
    )
    fetched, incoming = (replies, incoming)
    cache = fetched[target, slot_of]
    coef = factors[blocks]
    halfway = jnp.einsum("xpi,xyij->xypj", coef, cache, preferred_element_type=jnp.float32).astype(
        jnp.bfloat16
    )
    pair_diag = jnp.einsum("xypj,ypj->xyp", halfway, coef, preferred_element_type=jnp.float32)

    def pair_row(row_half):
        return jnp.einsum(
            "ypj,yqj->ypq", row_half, coef, preferred_element_type=jnp.float32
        ).astype(jnp.bfloat16)

    pairwise = lax.map(pair_row, halfway)
    live = (jnp.arange(quartets.shape[0], dtype=jnp.int32) < count).astype(jnp.float32)
    first = quartets[:, 0]
    second = quartets[:, 1]
    third = quartets[:, 2]
    fourth = quartets[:, 3]
    coulomb_coef = pair_table(
        jnp.concatenate([first * ntask + second, third * ntask + fourth]),
        jnp.concatenate([third * ntask + fourth, first * ntask + second]),
        jnp.concatenate([2.0 * live, 2.0 * live]),
        npairs,
    )
    exchange_coef = pair_table(
        jnp.concatenate(
            [
                first * ntask + third,
                first * ntask + fourth,
                second * ntask + third,
                second * ntask + fourth,
            ]
        ),
        jnp.concatenate(
            [
                second * ntask + fourth,
                second * ntask + third,
                first * ntask + fourth,
                first * ntask + third,
            ]
        ),
        jnp.concatenate([-0.5 * live, -0.5 * live, -0.5 * live, -0.5 * live]),
        npairs,
    )
    coulomb_sum = jnp.dot(
        coulomb_coef, pair_diag.reshape(npairs, points), precision=lax.Precision.HIGHEST
    )
    coulomb_pot = jnp.dot(coulomb_sum, core, precision=lax.Precision.HIGHEST)
    exchange_table = exchange_coef.astype(jnp.bfloat16)
    flat_pairs = pairwise.reshape(npairs, points * points)
    identity = jnp.eye(points, dtype=jnp.float32)
    group_rows = 4
    group_pairs = group_rows * ntask

    def target_group(number):
        start = number * group_pairs
        table_rows = lax.dynamic_slice_in_dim(exchange_table, start, group_pairs, 0)
        potential = lax.dynamic_slice_in_dim(coulomb_pot, start, group_pairs, 0)
        rows_coef = lax.dynamic_slice_in_dim(coef, number * group_rows, group_rows, 0)
        exchange_sum = jnp.dot(table_rows, flat_pairs, preferred_element_type=jnp.float32).reshape(
            group_pairs, points, points
        )
        core_matrix = (core[None] * exchange_sum + identity[None] * potential[:, :, None]).astype(
            jnp.bfloat16
        )
        core_matrix = core_matrix.reshape(group_rows, ntask, points, points)
        right_half = jnp.einsum(
            "xypq,yqj->xypj", core_matrix, coef, preferred_element_type=jnp.float32
        ).astype(jnp.bfloat16)
        return jnp.einsum(
            "xpi,xypj->xyij", rows_coef, right_half, preferred_element_type=jnp.float32
        ).astype(jnp.bfloat16)

    pieces = lax.map(target_group, jnp.arange(ntask // group_rows, dtype=jnp.int32)).reshape(
        npairs, width, width
    )
    outbound = jnp.zeros((devices, slots, width, width), jnp.bfloat16)
    outbound = outbound.at[target.reshape(-1), slot_of.reshape(-1)].set(pieces)
    inbound = lax.all_to_all(outbound, ("row", "bulk"), split_axis=0, concat_axis=0, tiled=True)
    valid, local_row, local_col = local_place(incoming)
    place = (local_row * col_blocks + local_col).reshape(-1)
    contrib = jnp.where(
        valid[:, :, None, None], inbound.astype(jnp.float32), jnp.zeros((), jnp.float32)
    ).reshape(-1, width, width)
    fock = jnp.zeros((row_blocks * col_blocks, width, width), jnp.float32).at[place].add(contrib)
    return fock.reshape(row_blocks, col_blocks, width, width)


def solution(mesh):
    return jax.shard_map(
        shards,
        mesh=mesh,
        in_specs=(
            P("row", "bulk", None, None),
            P(),
            P(),
            P(("row", "bulk"), None),
            P(("row", "bulk"), None),
            P(("row", "bulk")),
        ),
        out_specs=P("row", "bulk", None, None),
        check_vma=False,
    )
```

profile of v0, /device:TPU:90, one launch (start us, length us, event | category | flops | bytes accessed | tf_op | source)
XLA Modules:
  0.0 911.3 jit_solution(3926874356994909528)
XLA Ops:
  3.5 7.8 scatter_fusion
  12.8 9.9 %all-to-all-start = ((s32[128,3,2]{1,2,0:T(2,128)}), s32[128,3,2]{1,2,0:T(2,128)S(1)}, u32[]{:S(2)}, u32[]{:S(2)}) async-start(s32[128,3,2]{1,2,0:T(2,128)} %copy.19), calls=%async_computation | async-start | bytes 262144 | tf_op jit(solution)/shard_map/all_to_all | solution.py:44
  22.7 4.9 all-to-all-done
  29.6 16.2 %gather_fusion = bf16[384,128,128]{2,1,0:T(8,128)(2,1)} fusion(bf16[24,3,128,128]{3,2,1,0:T(8,128)(2,1)S(1)} %copy-done, s32[384]{0:T(512)S(1)} %reshape.501), kind=kCustom, calls=%fused_computation | custom fusion | bytes 25168896 | tf_op jit(solution)/shard_map/gather | solution.py:46
  45.8 10.8 %broadcast_select_fusion = bf16[128,3,128,128]{3,2,1,0:T(8,128)(2,1)} fusion(bf16[128,3,128,128]{3,2,1,0:T(8,128)(2,1)} %bitcast.127, pred[128,3]{1,0:T(8,128)(4,1)S(1)} %copy.21), kind=kLoop, calls=%fused_computation.33 | loop fusion | flops 6291456 | bytes 25166208 | tf_op jit(solution)/shard_map/jit(_where)/select_n | solution.py:48
  56.6 10.5 %all-to-all-start.1 = ((bf16[128,3,128,128]{3,2,1,0:T(8,128)(2,1)}), bf16[128,3,128,128]{3,2,1,0:T(8,128)(2,1)}, u32[]{:S(2)}, u32[]{:S(2)}) async-start(bf16[128,3,128,128]{3,2,1,0:T(8,128)(2,1)} %broadcast_select_fusion), calls=%async_computation.1 | async-start | bytes 25165824 | tf_op jit(solution)/shard_map/all_to_all | solution.py:47
  67.3 4.5 gather_fusion.2
  75.7 159.8 %all-to-all-done.1 = bf16[128,3,128,128]{3,2,1,0:T(8,128)(2,1)} async-done(((bf16[128,3,128,128]{3,2,1,0:T(8,128)(2,1)}), bf16[128,3,128,128]{3,2,1,0:T(8,128)(2,1)}, u32[]{:S(2)}, u32[]{:S(2)}) %all-to-all-start.1) | async-done | bytes 12582944 | tf_op jit(solution)/shard_map/all_to_all | solution.py:47
  235.5 16.7 %gather_fusion.1 = bf16[144,128,128]{2,1,0:T(8,128)(2,1)} fusion(bf16[128,3,128,128]{3,2,1,0:T(8,128)(2,1)} %all-to-all-done.1, s32[144]{0:T(256)S(1)} %reshape.507), kind=kCustom, calls=%fused_computation.1 | custom fusion | bytes 9438336 | tf_op jit(solution)/shard_map/gather | solution.py:55
  252.2 11.5 %multiply_reduce_fusion = (f32[12,384,12]{1,0,2:T(8,128)S(1)}, bf16[12,12,128,384]{3,2,1,0:T(8,128)(2,1)}) fusion(f32[12,384,128]{1,2,0:T(8,128)} %copy.36, bf16[12,12,128,128]{3,2,1,0:T(8,128)(2,1)} %bitcast.129, bf16[12,384,128]{2,1,0:T(8,128)(2,1)S(1)} %gather_fusion.2), kind=kOutput, calls=%fused_computation.31 | convolution fusion | flops 1840195584 | bytes 22634496 | tf_op jit(solution)/shard_map/xpi,xyij->xypj/dot_general | solution.py:57
  263.7 50.2 %while.21 = (s32[]{:T(128)}, bf16[12,12,384,384]{3,2,1,0:T(8,128)(2,1)}, bf16[12,12,384,128]{2,3,1,0:T(8,128)(2,1)}, bf16[12,384,128]{2,1,0:T(8,128)(2,1)S(1)}, s32[]{:T(128)}) while((s32[]{:T(128)}, bf16[12,12,384,384]{3,2,1,0:T(8,128)(2,1)}, bf16[12,12,384,128]{2,3,1,0:T(8,128)(2,1)}, bf16[12,384,128]{2,1,0:T(8,128)(2,1)S(1)}, ...), condition=%wide.region_2.3_spmd, body=%wide.region_1.2_spmd.sunk | while | flops 454754304 | bytes 5899325 | solution.py:67
  284.5 4.2 bitcast_dynamic-update-slice_fusion.4
  301.2 4.2 bitcast_dynamic-update-slice_fusion.4
  305.4 4.3 bitcast_dynamic-update-slice_fusion.4
  313.9 84.1 %copy.39 = bf16[18,8,384,384]{3,1,2,0:T(8,128)(2,1)} copy(bf16[18,8,384,384]{3,2,1,0:T(8,128)(2,1)} %bitcast.128) | data formatting | bytes 84934656
  399.1 198.6 %while.22 = (s32[]{:T(128)}, bf16[3,4,12,128,128]{3,4,2,1,0:T(8,128)(2,1)}, f32[384,384]{1,0:T(8,128)S(1)}, s32[3]{0:T(128)S(1)}, bf16[144,144]{1,0:T(8,128)(2,1...) while((s32[]{:T(128)}, ...), condition=%wide.region_4.5_spmd.clone, body=%wide.region_3.4_spmd.clone.sunk | while | flops 4486103040 | bytes 161047296 | solution.py:128
  400.3 25.7 %fusion.78 = f32[48,147456]{1,0:T(8,128)} fusion(bf16[144,147456]{1,0:T(8,128)(2,1)} %get-tuple-element.279, bf16[144,144]{1,0:T(8,128)(2,1)S(1)} %get-tuple-element.278, s32[]{:T(128)S(6)} %select_n.213), kind=kOutput, calls=%fused_computation.26.clone.1 | convolution fusion | flops 2038431744 | bytes 70803456 | tf_op jit(solution)/shard_map/while/body/eval_jaxpr/dot_general | solution.py:114
  426.0 25.4 %copy.41 = f32[6,8,384,384]{3,2,1,0:T(8,128)} copy(f32[6,8,384,384]{3,1,2,0:T(8,128)} %bitcast.122) | data formatting | bytes 56623104 | tf_op jit(solution)/shard_map/while
  452.0 13.3 %bitcast_dynamic-update-slice_fusion.5 = bf16[3,4,12,128,128]{3,4,2,1,0:T(8,128)(2,1)} fusion(bf16[3,4,12,128,128]{3,4,2,1,0:T(8,128)(2,1)} %get-tuple-element.261, s32[]{:T(128)} %get-tuple-element.260, f32[4,12,384,384]{3,2,1,0:T(8,128)} %bitcast.124, f32[4,12,384]{2,1,0:T(8,128)S(1)} %mul.264, f32[384,384]{1,0:T(8,128)S(1)} %fusion.79, ...), kind=kOutput, calls=%fused_computation.20.clone.1 | convolution fusion | flops 2447376384 | bytes 32735748 | tf_op jit(solution)/shard_map/while/body/eval_jaxpr/xpi,xypj->xyij/dot_general | solution.py:124
  466.5 25.7 %fusion.78 = f32[48,147456]{1,0:T(8,128)} fusion(bf16[144,147456]{1,0:T(8,128)(2,1)} %get-tuple-element.279, bf16[144,144]{1,0:T(8,128)(2,1)S(1)} %get-tuple-element.278, s32[]{:T(128)S(6)} %select_n.213), kind=kOutput, calls=%fused_computation.26.clone.1 | convolution fusion | flops 2038431744 | bytes 70803456 | tf_op jit(solution)/shard_map/while/body/eval_jaxpr/dot_general | solution.py:114
  492.2 25.4 %copy.41 = f32[6,8,384,384]{3,2,1,0:T(8,128)} copy(f32[6,8,384,384]{3,1,2,0:T(8,128)} %bitcast.122) | data formatting | bytes 56623104 | tf_op jit(solution)/shard_map/while
  518.2 13.3 %bitcast_dynamic-update-slice_fusion.5 = bf16[3,4,12,128,128]{3,4,2,1,0:T(8,128)(2,1)} fusion(bf16[3,4,12,128,128]{3,4,2,1,0:T(8,128)(2,1)} %get-tuple-element.261, s32[]{:T(128)} %get-tuple-element.260, f32[4,12,384,384]{3,2,1,0:T(8,128)} %bitcast.124, f32[4,12,384]{2,1,0:T(8,128)S(1)} %mul.264, f32[384,384]{1,0:T(8,128)S(1)} %fusion.79, ...), kind=kOutput, calls=%fused_computation.20.clone.1 | convolution fusion | flops 2447376384 | bytes 32735748 | tf_op jit(solution)/shard_map/while/body/eval_jaxpr/xpi,xypj->xyij/dot_general | solution.py:124
  532.7 25.7 %fusion.78 = f32[48,147456]{1,0:T(8,128)} fusion(bf16[144,147456]{1,0:T(8,128)(2,1)} %get-tuple-element.279, bf16[144,144]{1,0:T(8,128)(2,1)S(1)} %get-tuple-element.278, s32[]{:T(128)S(6)} %select_n.213), kind=kOutput, calls=%fused_computation.26.clone.1 | convolution fusion | flops 2038431744 | bytes 70803456 | tf_op jit(solution)/shard_map/while/body/eval_jaxpr/dot_general | solution.py:114
  558.4 25.4 %copy.41 = f32[6,8,384,384]{3,2,1,0:T(8,128)} copy(f32[6,8,384,384]{3,1,2,0:T(8,128)} %bitcast.122) | data formatting | bytes 56623104 | tf_op jit(solution)/shard_map/while
  584.4 13.3 %bitcast_dynamic-update-slice_fusion.5 = bf16[3,4,12,128,128]{3,4,2,1,0:T(8,128)(2,1)} fusion(bf16[3,4,12,128,128]{3,4,2,1,0:T(8,128)(2,1)} %get-tuple-element.261, s32[]{:T(128)} %get-tuple-element.260, f32[4,12,384,384]{3,2,1,0:T(8,128)} %bitcast.124, f32[4,12,384]{2,1,0:T(8,128)S(1)} %mul.264, f32[384,384]{1,0:T(8,128)S(1)} %fusion.79, ...), kind=kOutput, calls=%fused_computation.20.clone.1 | convolution fusion | flops 2447376384 | bytes 32735748 | tf_op jit(solution)/shard_map/while/body/eval_jaxpr/xpi,xypj->xyij/dot_general | solution.py:124
  597.7 6.7 copy.24
  604.4 7.7 broadcast.509
  612.1 23.5 %scatter_fusion.1 = bf16[128,3,128,128]{3,2,1,0:T(8,128)(2,1)} fusion(bf16[128,3,128,128]{3,2,1,0:T(8,128)(2,1)} %broadcast.509, s32[144]{0:T(256)S(1)} %bitcast.131, bf16[144,128,128]{2,1,0:T(8,128)(2,1)} %copy.24), kind=kCustom, calls=%fused_computation.4 | custom fusion | bytes 14156928 | tf_op jit(solution)/shard_map/scatter | solution.py:132
  635.6 10.2 %all-to-all-start.2 = ((bf16[128,3,128,128]{3,2,1,0:T(8,128)(2,1)}), bf16[128,3,128,128]{3,2,1,0:T(8,128)(2,1)}, u32[]{:S(2)}, u32[]{:S(2)}) async-start(bf16[128,3,128,128]{3,2,1,0:T(8,128)(2,1)} %scatter_fusion.1), calls=%async_computation.2 | async-start | bytes 25165824 | tf_op jit(solution)/shard_map/all_to_all | solution.py:133
  646.0 168.9 %all-to-all-done.2 = bf16[128,3,128,128]{3,2,1,0:T(8,128)(2,1)} async-done(((bf16[128,3,128,128]{3,2,1,0:T(8,128)(2,1)}), bf16[128,3,128,128]{3,2,1,0:T(8,128)(2,1)}, u32[]{:S(2)}, u32[]{:S(2)}) %all-to-all-start.2) | async-done | bytes 12582944 | tf_op jit(solution)/shard_map/all_to_all | solution.py:133
  814.9 14.2 %convert_select_fusion = f32[128,3,128,128]{3,2,1,0:T(8,128)} fusion(bf16[128,3,128,128]{3,2,1,0:T(8,128)(2,1)} %all-to-all-done.2, pred[128,3]{1,0:T(8,128)(4,1)S(1)} %copy-done.7), kind=kLoop, calls=%fused_computation.32 | loop fusion | flops 12582912 | bytes 37749120 | tf_op jit(solution)/shard_map/jit(_where)/select_n | solution.py:136
  831.9 79.4 %scatter_fusion.2 = f32[72,128,128]{2,1,0:T(8,128)} fusion(f32[72,128,128]{2,1,0:T(8,128)} %broadcast_in_dim.107, s32[384]{0:T(512)S(1)} %fusion.48, f32[384,128,128]{2,1,0:T(8,128)} %bitcast.125), kind=kCustom, calls=%fused_computation.5 | custom fusion | flops 6291456 | bytes 75499008 | tf_op jit(solution)/shard_map/scatter-add | solution.py:139
  (83 shorter events, 53.7 us)
Async XLA Ops:
  0.0 29.6 %copy-start = (bf16[24,3,128,128]{3,2,1,0:T(8,128)(2,1)S(1)}, bf16[24,3,128,128]{3,2,1,0:T(8,128)(2,1)}, u32[]{:S(2)}) copy-start(bf16[24,3,128,128]{3,2,1,0:T(8,128)(2,1)} %param.10) | copy-start | bytes 7077892
  3.4 25.6 %copy-start.2 = (s32[144,1]{0,1:T(1,128)}, s32[144,1]{0,1:T(1,128)S(1)}, u32[]{:S(2)}) copy-start(s32[144,1]{0,1:T(1,128)S(1)} %or_select_fusion) | copy-start | bytes 1732
  12.8 14.8 %all-to-all-start = ((s32[128,3,2]{1,2,0:T(2,128)}), s32[128,3,2]{1,2,0:T(2,128)S(1)}, u32[]{:S(2)}, u32[]{:S(2)}) async-start(s32[128,3,2]{1,2,0:T(2,128)} %copy.19), calls=%async_computation | async-start | bytes 262144 | tf_op jit(solution)/shard_map/all_to_all | solution.py:44
  29.6 16.2 %copy-start.6 = (pred[128,3]{1,0:T(8,128)(4,1)}, pred[128,3]{1,0:T(8,128)(4,1)S(1)}, u32[]{:S(2)}) copy-start(pred[128,3]{1,0:T(8,128)(4,1)S(1)} %copy.21) | copy-start | bytes 1156
  56.6 10.7 %copy-start.8 = (s32[1,12]{1,0:T(1,128)S(1)}, s32[1,12]{1,0:T(1,128)}, u32[]{:S(2)}) copy-start(s32[1,12]{1,0:T(1,128)} %param.13) | copy-start | bytes 148
  56.6 17.7 %copy-start.9 = (s32[128,4]{0,1:T(4,128)S(1)}, s32[128,4]{0,1:T(4,128)}, u32[]{:S(2)}) copy-start(s32[128,4]{0,1:T(4,128)} %param.14) | copy-start | bytes 6148
  56.6 178.8 %all-to-all-start.1 = ((bf16[128,3,128,128]{3,2,1,0:T(8,128)(2,1)}), bf16[128,3,128,128]{3,2,1,0:T(8,128)(2,1)}, u32[]{:S(2)}, u32[]{:S(2)}) async-start(bf16[128,3,128,128]{3,2,1,0:T(8,128)(2,1)} %broadcast_select_fusion), calls=%async_computation.1 | async-start | bytes 25165824 | tf_op jit(solution)/shard_map/all_to_all | solution.py:47
  313.9 84.5 %copy-start.4 = (f32[384,384]{1,0:T(8,128)S(1)}, f32[384,384]{1,0:T(8,128)}, u32[]{:S(2)}) copy-start(f32[384,384]{1,0:T(8,128)} %param.12) | copy-start | bytes 1769476
  597.7 14.4 %copy-start.3 = (s32[144,1]{0,1:T(1,128)S(1)}, s32[144,1]{0,1:T(1,128)}, u32[]{:S(2)}) copy-start(s32[144,1]{0,1:T(1,128)} %copy-done.2) | copy-start | bytes 1732
  635.6 10.2 %copy-start.5 = (s32[128,3]{1,0:T(8,128)S(1)}, s32[128,3]{1,0:T(8,128)}, u32[]{:S(2)}) copy-start(s32[128,3]{1,0:T(8,128)} %get-tuple-element.107) | copy-start | bytes 4612
  635.6 179.3 %copy-start.7 = (pred[128,3]{1,0:T(8,128)(4,1)S(1)}, pred[128,3]{1,0:T(8,128)(4,1)}, u32[]{:S(2)}) copy-start(pred[128,3]{1,0:T(8,128)(4,1)} %copy-done.6) | copy-start | bytes 1156
  635.6 179.3 %all-to-all-start.2 = ((bf16[128,3,128,128]{3,2,1,0:T(8,128)(2,1)}), bf16[128,3,128,128]{3,2,1,0:T(8,128)(2,1)}, u32[]{:S(2)}, u32[]{:S(2)}) async-start(bf16[128,3,128,128]{3,2,1,0:T(8,128)(2,1)} %scatter_fusion.1), calls=%async_computation.2 | async-start | bytes 25165824 | tf_op jit(solution)/shard_map/all_to_all | solution.py:133
  831.9 79.4 %copy-start.1 = (bf16[24,3,128,128]{3,2,1,0:T(8,128)(2,1)S(1)}, bf16[24,3,128,128]{3,2,1,0:T(8,128)(2,1)}, u32[]{:S(2)}) copy-start(bf16[24,3,128,128]{3,2,1,0:T(8,128)(2,1)} %param.10) | copy-start | bytes 7077892
where the time goes:
time: 914 us; the launch traced here: 911 us
  waiting for transfers between devices  334 us (37%)
  local copies, waits for them, and re-layouts  254 us (28%)
  matrix products  181 us (20%)
  other arithmetic  108 us (12%)
  starting transfers between devices  30.5 us (3%)
    all_to_all x1, waiting for transfers between devices, shards(): lax.all_to_all(outbound, ('row', 'bulk'), split_axis=0, concat_axis=0, ti...  169 us
    all_to_all x1, waiting for transfers between devices, shards(): lax.all_to_all(jnp.where(valid[:, :, None, None], found, jnp.zeros_like(f...  160 us
    unnamed x22, local copies, waits for them, and re-layouts  86 us
    scatter-add x1, other arithmetic, shards(): jnp.zeros((row_blocks * col_blocks, width, width), jnp.float32).at[place]  79.4 us
    dot_general x3, matrix products, target_group(): jnp.dot(table_rows, flat_pairs, preferred_element_type=jnp.float32)  77 us
    while x3, local copies, waits for them, and re-layouts  76.1 us
    dot_general x12, matrix products, pair_row(): jnp.einsum('ypj,yqj->ypq', row_half, coef, preferred_element_type=jnp.flo...  50.2 us
    dot_general x3, matrix products, target_group(): jnp.einsum('xpi,xypj->xyij', rows_coef, right_half, preferred_element_typ...  39.9 us
  transfers between devices with their start and end apart: 3, of which 3 were waited for; matrix products, arithmetic and copies ran while one was open for 1% of the time, Pallas kernels for 0%

commit v1 on v0

v1 whole, which is shorter than its diff:
```python
import jax
import jax.numpy as jnp
from jax import lax
from jax.experimental import pallas as pl
from jax.experimental.pallas import tpu as pltpu
from jax.sharding import PartitionSpec as P

T = 12
NP = 144
R = 384
BS = 128
CAPE = 512


def entries_kernel(quads, count, lst, start, nxt):
    live = count[0]

    def zero(i, c):
        start[i] = 0
        return c

    lax.fori_loop(0, NP + 1, zero, 0)

    def quad(i):
        return quads[4 * i], quads[4 * i + 1], quads[4 * i + 2], quads[4 * i + 3]

    def add(t):
        start[t + 1] = start[t + 1] + 1

    def tally(i, c):
        a, b, d, e = quad(i)
        add(a * T + d)
        add(a * T + e)
        add(b * T + d)
        add(b * T + e)
        return c

    lax.fori_loop(0, live, tally, 0)

    def running(i, total):
        total = total + start[i + 1]
        start[i + 1] = total
        nxt[i + 1] = total
        return total

    nxt[0] = 0
    lax.fori_loop(0, NP, running, 0)

    def fill(i, c):
        lst[i] = NP
        return c

    lax.fori_loop(0, lst.shape[0], fill, 0)

    def put(t, s):
        at = nxt[t]
        lst[at] = s
        nxt[t] = at + 1

    def place(i, c):
        a, b, d, e = quad(i)
        put(a * T + d, b * T + e)
        put(a * T + e, b * T + d)
        put(b * T + d, a * T + e)
        put(b * T + e, a * T + d)
        return c

    lax.fori_loop(0, live, place, 0)


def entries(quads, count):
    smem = pl.BlockSpec(memory_space=pltpu.SMEM)
    return pl.pallas_call(
        entries_kernel,
        out_shape=[
            jax.ShapeDtypeStruct((CAPE + 128,), jnp.int32),
            jax.ShapeDtypeStruct((256,), jnp.int32),
        ],
        in_specs=[smem, smem],
        out_specs=[smem, smem],
        scratch_shapes=[pltpu.SMEM((256,), jnp.int32)],
        cost_estimate=pl.CostEstimate(flops=10000, bytes_accessed=10000, transcendentals=0),
        name="sort_entries",
    )(quads.reshape(-1), count)


def compute_kernel(ids, in_slot, out_slot, lst, start, core, coul, recv, factors, outbound,
                   dens, fac, fact, half, pieces, pdt, corem, pot, acc, in_sem, fac_sem, out_sem):
    for x in range(T):
        pltpu.make_async_copy(factors.at[ids[x]], fac.at[x], fac_sem).start()
    for x in range(T):
        def fetch(y, c, x=x):
            pltpu.make_async_copy(recv.at[in_slot[x * T + y]], dens.at[x * T + y], in_sem.at[x]).start()
            return c
        lax.fori_loop(0, T, fetch, 0)
    corem[...] = core[...] * -0.5
    half[NP] = jnp.zeros((R, BS), jnp.bfloat16)
    pdt[...] = jnp.zeros_like(pdt)
    pltpu.make_async_copy(factors.at[pl.ds(0, T)], fac, fac_sem).wait()
    for x in range(T):
        fact[x] = fac[x].T

    rowk = lax.broadcasted_iota(jnp.int32, (2 * BS, 256), 0) // BS
    cols = lax.broadcasted_iota(jnp.int32, (2 * BS, 256), 1)
    delta = cols - rowk

    def halves(x, c):
        pltpu.make_async_copy(recv.at[pl.ds(0, T)], dens.at[pl.ds(0, T)], in_sem.at[x]).wait()
        fx = fac[x]
        for yp in range(T // 2):
            s = x * T + 2 * yp
            d2 = jnp.concatenate([dens[s], dens[s + 1]], axis=1)
            h2 = jnp.dot(fx, d2, preferred_element_type=jnp.float32).astype(jnp.bfloat16)
            half[s] = h2[:, :BS]
            half[s + 1] = h2[:, BS:]
            f2 = jnp.concatenate([fac[2 * yp], fac[2 * yp + 1]], axis=1)
            prod = (h2.astype(jnp.float32) * f2.astype(jnp.float32)).astype(jnp.bfloat16)
            spread = (delta == s).astype(jnp.bfloat16)
            pdt[...] += jnp.dot(prod, spread, preferred_element_type=jnp.float32)
        return c

    lax.fori_loop(0, T, halves, 0)
    pair_diag = pdt[...].T
    total = jnp.dot(coul[...], pair_diag, precision=lax.Precision.HIGHEST, preferred_element_type=jnp.float32)
    pot[...] = jnp.dot(total, core[...], precision=lax.Precision.HIGHEST, preferred_element_type=jnp.float32).reshape(NP, 1, R)
    eye = lax.broadcasted_iota(jnp.int32, (BS, BS), 0) == lax.broadcasted_iota(jnp.int32, (BS, BS), 1)

    def target(t, c):
        x = t // T
        y = t % T
        lo = start[t]
        n = (start[t + 1] - lo)

        def pair(k):
            s1 = lst[lo + 2 * k]
            s2 = jnp.where(2 * k + 1 < n, lst[lo + 2 * k + 1], NP)
            y1 = lax.rem(s1, T)
            y2 = lax.rem(s2, T)
            h = jnp.concatenate([half[s1], half[s2]], axis=1)
            w = jnp.concatenate([fact[y1], fact[y2]], axis=0)
            return jnp.dot(h, w, preferred_element_type=jnp.float32)

        acc[...] = jnp.zeros_like(acc)

        def more(k, c):
            acc[...] += pair(k)
            return c

        lax.fori_loop(0, (n + 1) // 2, more, 0)
        row = pot[t]
        cm = corem[...] * acc[...]
        parts = []
        for k in range(3):
            line = cm[k * BS:(k + 1) * BS]
            blk = line[:, k * BS:(k + 1) * BS] + jnp.where(eye, row[:, k * BS:(k + 1) * BS], 0.0)
            cols3 = [line[:, j * BS:(j + 1) * BS] for j in range(3)]
            cols3[k] = blk
            parts.append(jnp.concatenate(cols3, axis=1))
        cm = jnp.concatenate(parts, axis=0).astype(jnp.bfloat16)
        rh = jnp.dot(cm, fac[y], preferred_element_type=jnp.float32).astype(jnp.bfloat16)
        pieces[t] = jnp.dot(fact[x], rh, preferred_element_type=jnp.float32).astype(jnp.bfloat16)
        pltpu.make_async_copy(pieces.at[t], outbound.at[out_slot[t]], out_sem).start()
        return c

    lax.fori_loop(0, NP, target, 0)
    pltpu.make_async_copy(pieces, outbound.at[pl.ds(0, NP)], out_sem).wait()


def compute(ids, in_slot, out_slot, lst, start, core, coul, recv, factors, nslots, kernel=compute_kernel):
    smem = pl.BlockSpec(memory_space=pltpu.SMEM)
    vmem = pl.BlockSpec(memory_space=pltpu.VMEM)
    hbm = pl.BlockSpec(memory_space=pl.ANY)
    return pl.pallas_call(
        kernel,
        out_shape=jax.ShapeDtypeStruct((nslots, BS, BS), jnp.bfloat16),
        in_specs=[smem] * 5 + [vmem] * 2 + [hbm] * 2,
        out_specs=hbm,
        scratch_shapes=[
            pltpu.VMEM((NP, BS, BS), jnp.bfloat16),
            pltpu.VMEM((T, R, BS), jnp.bfloat16),
            pltpu.VMEM((T, BS, R), jnp.bfloat16),
            pltpu.VMEM((NP + 1, R, BS), jnp.bfloat16),
            pltpu.VMEM((NP, BS, BS), jnp.bfloat16),
            pltpu.VMEM((R, 256), jnp.float32),
            pltpu.VMEM((R, R), jnp.float32),
            pltpu.VMEM((NP, 1, R), jnp.float32),
            pltpu.VMEM((R, R), jnp.float32),
            pltpu.SemaphoreType.DMA((T,)),
            pltpu.SemaphoreType.DMA,
            pltpu.SemaphoreType.DMA,
        ],
        compiler_params=pltpu.CompilerParams(vmem_limit_bytes=50 * 2**20),
        cost_estimate=pl.CostEstimate(flops=25 * 10**9, bytes_accessed=12 * 10**6, transcendentals=0),
        name="fock_pieces",
    )(ids, in_slot, out_slot, lst, start, core, coul, recv, factors)


def coulomb_table(quads, count):
    live = (jnp.arange(128, dtype=jnp.int32) < count).astype(jnp.float32)
    p = quads[:, 0] * T + quads[:, 1]
    q = quads[:, 2] * T + quads[:, 3]
    tg = jnp.concatenate([p, q])
    sr = jnp.concatenate([q, p])
    ht = (tg[:, None] == jnp.arange(NP)[None]).astype(jnp.bfloat16)
    hs = jnp.where(sr[:, None] == jnp.arange(256)[None], jnp.concatenate([live, live])[:, None] * 2.0, 0.0).astype(jnp.bfloat16)
    return lax.dot_general(ht, hs, (((0,), (0,)), ((), ())), preferred_element_type=jnp.float32)


def column_of(ids, d, bulk):
    group = bulk // 8
    local = jnp.int32(-1)
    for j in range(3):
        block = ids[d * T + group * 3 + j]
        local = jnp.where(block // 3 == bulk, block % 3, local)
    return local


def pack_kernel(place, ids, density, out, sem):
    row = place[0]
    bulk = place[1]

    def copy(d, j, col):
        r = ids[d * T + row * 3 + j] - row * 24
        return pltpu.make_async_copy(density.at[r, col], out.at[d * 3 + j], sem)

    def send(d, n):
        col = column_of(ids, d, bulk)

        @pl.when(col >= 0)
        def _():
            for j in range(3):
                copy(d, j, col).start()

        return n + (col >= 0).astype(jnp.int32)

    n = lax.fori_loop(0, 128, send, 0)

    def drain(i, c):
        pltpu.make_async_copy(out.at[pl.ds(0, 3)], out.at[pl.ds(0, 3)], sem).wait()
        return c

    lax.fori_loop(0, n, drain, 0)


def pack(place, ids, density):
    smem = pl.BlockSpec(memory_space=pltpu.SMEM)
    hbm = pl.BlockSpec(memory_space=pl.ANY)
    return pl.pallas_call(
        pack_kernel,
        out_shape=jax.ShapeDtypeStruct((384, BS, BS), jnp.bfloat16),
        in_specs=[smem, smem, hbm],
        out_specs=hbm,
        scratch_shapes=[pltpu.SemaphoreType.DMA],
        name="pack_density",
    )(place, ids, density)


def gather_kernel(place, ids, inbound, fock, buf, sems):
    row = place[0]
    bulk = place[1]

    def fetch(d, c):
        @pl.when(column_of(ids, d, bulk) >= 0)
        def _():
            pltpu.make_async_copy(inbound.at[pl.ds(d * 3, 3)], buf.at[pl.ds(d * 3, 3)], sems.at[d]).start()

        return c

    lax.fori_loop(0, 128, fetch, 0)
    fock[...] = jnp.zeros_like(fock)

    def add(d, c):
        col = column_of(ids, d, bulk)

        @pl.when(col >= 0)
        def _():
            pltpu.make_async_copy(inbound.at[pl.ds(d * 3, 3)], buf.at[pl.ds(d * 3, 3)], sems.at[d]).wait()
            for j in range(3):
                r = ids[d * T + row * 3 + j] - row * 24
                fock[r, col] += buf[d * 3 + j].astype(jnp.float32)

        return c

    lax.fori_loop(0, 128, add, 0)


def gather(place, ids, inbound):
    smem = pl.BlockSpec(memory_space=pltpu.SMEM)
    vmem = pl.BlockSpec(memory_space=pltpu.VMEM)
    hbm = pl.BlockSpec(memory_space=pl.ANY)
    return pl.pallas_call(
        gather_kernel,
        out_shape=jax.ShapeDtypeStruct((24, 3, BS, BS), jnp.float32),
        in_specs=[smem, smem, hbm],
        out_specs=vmem,
        scratch_shapes=[pltpu.VMEM((384, BS, BS), jnp.bfloat16), pltpu.SemaphoreType.DMA((128,))],
        compiler_params=pltpu.CompilerParams(vmem_limit_bytes=40 * 2**20),
        name="add_pieces",
    )(place, ids, inbound)


def shards(density, factors, core, task_blocks, quartets, quartet_count):
    axes = ("row", "bulk")
    mine = task_blocks[0]
    place = jnp.stack([lax.axis_index("row"), lax.axis_index("bulk")]).astype(jnp.int32)
    ids = lax.all_to_all(
        jnp.broadcast_to(mine[None], (128, T)), axes, split_axis=0, concat_axis=0, tiled=True
    ).reshape(-1)
    sent = pack(place, ids, density)
    recv = lax.all_to_all(sent, axes, split_axis=0, concat_axis=0, tiled=True)
    lst, start = entries(quartets, quartet_count)
    coul = coulomb_table(quartets, quartet_count[0])
    owner = mine[:, None] // 24 * 32 + mine[None, :] // 3
    slot = (owner * 3 + (jnp.arange(T) % 3)[:, None]).reshape(-1).astype(jnp.int32)
    outbound = compute(mine, slot, slot, lst, start, core, coul, recv, factors, 384)
    inbound = lax.all_to_all(outbound, axes, split_axis=0, concat_axis=0, tiled=True)
    return gather(place, ids, inbound)


def solution(mesh):
    return jax.shard_map(
        shards,
        mesh=mesh,
        in_specs=(
            P("row", "bulk", None, None),
            P(),
            P(),
            P(("row", "bulk"), None),
            P(("row", "bulk"), None),
            P(("row", "bulk")),
        ),
        out_specs=P("row", "bulk", None, None),
        check_vma=False,
    )
```

time: 914 us -> 711 us (0.78)
  the two profiles are of different devices: /device:TPU:90 before, /device:TPU:1 now
where the time goes in v1:
time: 711 us; the launch traced here: 710 us
  Pallas kernels  274 us (39%)
  blocking collectives  238 us (33%)
  waiting for transfers between devices  151 us (21%)
  starting transfers between devices  39.8 us (6%)
    all_to_all x1, blocking collectives, shards(): lax.all_to_all(outbound, axes, split_axis=0, concat_axis=0, tiled=True)  238 us
    pallas_call x1, Pallas kernels, pack(): pl.pallas_call(pack_kernel, out_shape=jax.ShapeDtypeStruct((384, BS, BS),...  157 us
    all_to_all x1, waiting for transfers between devices, shards(): recv = lax.all_to_all(sent, axes, split_axis=0, concat_axis=0, tiled=True)  142 us
    pallas_call x1, Pallas kernels, compute(): pl.pallas_call(kernel, out_shape=jax.ShapeDtypeStruct((nslots, BS, BS), j...  87.8 us
    all_to_all x1, starting transfers between devices, shards(): recv = lax.all_to_all(sent, axes, split_axis=0, concat_axis=0, tiled=True)  28.3 us
    pallas_call x1, Pallas kernels, gather(): pl.pallas_call(gather_kernel, out_shape=jax.ShapeDtypeStruct((24, 3, BS,...  22.2 us
  transfers between devices with their start and end apart: 2, of which 2 were waited for; matrix products, arithmetic and copies ran while one was open for 0% of the time, Pallas kernels for 1%

profile of v1, /device:TPU:1, one launch (start us, length us, event | category | flops | bytes accessed | tf_op | source)
XLA Modules:
  0.0 710.2 jit_solution(819295562140799226)
XLA Ops:
  0.0 1.3 broadcast_in_dim.10
  1.3 11.5 %all-to-all-start = ((s32[128,1,12]{2,1,0:T(1,128)}), s32[128,1,12]{2,1,0:T(1,128)S(1)}, u32[]{:S(2)}, u32[]{:S(2)}) async-start(s32[128,1,12]{2,1,0:T(1,128)} %broadcast_in_dim.10), calls=%async_computation | async-start | bytes 131072 | tf_op jit(solution)/shard_map/all_to_all | solution.py:306
  12.8 0.7 pad_add_fusion.2.place
  13.5 8.9 %all-to-all-done = s32[128,1,12]{2,1,0:T(1,128)S(1)} async-done(((s32[128,1,12]{2,1,0:T(1,128)}), s32[128,1,12]{2,1,0:T(1,128)S(1)}, u32[]{:S(2)}, u32[]{:S(2)}) %all-to-all-start) | async-done | bytes 6176 | tf_op jit(solution)/shard_map/all_to_all | solution.py:306
  22.4 0.5 broadcast.100
  22.9 0.8 reduce.3
  23.7 0.7 reshape.84.ids
  24.4 156.8 %pack_density.1 = bf16[384,128,128]{2,1,0:T(8,128)(2,1)} custom-call(s32[2]{0:T(128)} %pad_add_fusion.2.place, s32[1536]{0:T(1024)} %reshape.84.ids, bf16[24,3,128,128]{3,2,1,0:T(8,128)(2,1)} %density.1), custom_call_target="tpu_custom_call" | custom-call | tf_op jit(solution)/shard_map/pack_density/pallas_call | solution.py:248
  181.2 0.0 copy-start.6
  181.2 0.0 copy-start.2
  181.2 0.0 copy-start.3
  181.2 28.3 %all-to-all-start.1 = ((bf16[384,128,128]{2,1,0:T(8,128)(2,1)}), bf16[384,128,128]{2,1,0:T(8,128)(2,1)}, u32[]{:S(2)}, u32[]{:S(2)}) async-start(bf16[384,128,128]{2,1,0:T(8,128)(2,1)} %pack_density.1), calls=%async_computation.1 | async-start | bytes 25165824 | tf_op jit(solution)/shard_map/all_to_all | solution.py:310
  210.2 0.0 copy-done.6
  210.2 0.1 copy.8
  210.3 0.7 reshape.85.quads
  211.0 7.3 %sort_entries.1 = (s32[640]{0:T(1024)}, s32[256]{0:T(256)}) custom-call(s32[512]{0:T(512)} %reshape.85.quads, s32[1]{0:T(128)} %copy.9.count), custom_call_target="tpu_custom_call" | custom-call | flops 10000 | bytes 10000 | tf_op jit(solution)/shard_map/sort_entries/pallas_call | solution.py:73
  218.3 0.0 copy-done.2
  218.3 0.1 multiply_add_fusion
  218.4 0.1 add.65.in_slot.out_slot
  218.6 0.3 fusion.coul
  218.9 142.2 %all-to-all-done.1.recv = bf16[384,128,128]{2,1,0:T(8,128)(2,1)} async-done(((bf16[384,128,128]{2,1,0:T(8,128)(2,1)}), bf16[384,128,128]{2,1,0:T(8,128)(2,1)}, u32[]{:S(2)}, u32[]{:S(2)}) %all-to-all-start.1) | async-done | bytes 12582944 | tf_op jit(solution)/shard_map/all_to_all | solution.py:310
  361.1 0.0 copy-done.3
  361.1 0.0 copy-start.4
  361.1 0.7 copy-done.4
  361.8 0.7 copy-done.5
  362.5 87.8 %fock_pieces.1 = bf16[384,128,128]{2,1,0:T(8,128)(2,1)} custom-call(s32[12]{0:T(128)S(1)} %bitcast.13, s32[144]{0:T(256)S(1)} %add.65.in_slot.out_slot, s32[144]{0:T(256)S(1)} %add.65.in_slot.out_slot, s32[640]{0:T(1024)S(1)} %copy-done.4, s32[256]{0:T(256)S(1)} %copy-done.5, f32[384,384]{1,0:T(8,128)S(1)} %copy-done.3, f32[144,256]{1,0:T(8,128)S(1)} %fusion.coul, ...), custom_call_target="tpu_custom_call" | custom-call | flops 24999999488 | bytes 12000000 | tf_op jit(solution)/shard_map/fock_pieces/pallas_call | solution.py:173
  450.3 0.0 copy-start
  450.3 0.0 copy-start.1
  450.3 237.7 %all_to_all.16.inbound = bf16[384,128,128]{2,1,0:T(8,128)(2,1)S(1)} all-to-all(bf16[384,128,128]{2,1,0:T(8,128)(2,1)} %fock_pieces.1), channel_id=1, replica_groups=mesh['row'=4,'bulk'=32] {'row','bulk'}, dimensions={0} | all-to-all | bytes 25165824 | tf_op jit(solution)/shard_map/all_to_all | solution.py:316
  688.0 0.0 copy-done
  688.0 0.0 copy-done.1
  688.0 22.2 %add_pieces.1 = f32[24,3,128,128]{3,2,1,0:T(8,128)} custom-call(s32[2]{0:T(128)S(1)} %copy-done.1, s32[1536]{0:T(1024)S(1)} %copy-done, bf16[384,128,128]{2,1,0:T(8,128)(2,1)S(1)} %all_to_all.16.inbound), custom_call_target="tpu_custom_call" | custom-call | tf_op jit(solution)/shard_map/add_pieces/pallas_call | solution.py:291
  (8 shorter events, 0.1 us)
Async XLA Ops:
  1.3 21.0 %all-to-all-start = ((s32[128,1,12]{2,1,0:T(1,128)}), s32[128,1,12]{2,1,0:T(1,128)S(1)}, u32[]{:S(2)}, u32[]{:S(2)}) async-start(s32[128,1,12]{2,1,0:T(1,128)} %broadcast_in_dim.10), calls=%async_computation | async-start | bytes 131072 | tf_op jit(solution)/shard_map/all_to_all | solution.py:306
  181.2 29.0 %copy-start.6 = (s32[128,4]{0,1:T(4,128)S(1)}, s32[128,4]{0,1:T(4,128)}, u32[]{:S(2)}) copy-start(s32[128,4]{0,1:T(4,128)} %param.10) | copy-start | bytes 6148
  181.2 37.1 %copy-start.2 = (s32[1,12]{1,0:T(1,128)S(1)}, s32[1,12]{1,0:T(1,128)}, u32[]{:S(2)}) copy-start(s32[1,12]{1,0:T(1,128)} %param.9) | copy-start | bytes 148
  181.2 180.0 %copy-start.3 = (f32[384,384]{1,0:T(8,128)S(1)}, f32[384,384]{1,0:T(8,128)}, u32[]{:S(2)}) copy-start(f32[384,384]{1,0:T(8,128)} %core.1) | copy-start | bytes 1769476
  181.2 179.9 %all-to-all-start.1 = ((bf16[384,128,128]{2,1,0:T(8,128)(2,1)}), bf16[384,128,128]{2,1,0:T(8,128)(2,1)}, u32[]{:S(2)}, u32[]{:S(2)}) async-start(bf16[384,128,128]{2,1,0:T(8,128)(2,1)} %pack_density.1), calls=%async_computation.1 | async-start | bytes 25165824 | tf_op jit(solution)/shard_map/all_to_all | solution.py:310
  361.1 0.7 copy-start.4
  361.8 0.7 copy-start.5
  450.3 237.7 %copy-start = (s32[1536]{0:T(1024)S(1)}, s32[1536]{0:T(1024)}, u32[]{:S(2)}) copy-start(s32[1536]{0:T(1024)} %reshape.84.ids) | copy-start | bytes 18436
  450.3 237.7 %copy-start.1 = (s32[2]{0:T(128)S(1)}, s32[2]{0:T(128)}, u32[]{:S(2)}) copy-start(s32[2]{0:T(128)} %pad_add_fusion.2.place) | copy-start | bytes 28

commit v2 on v1

--- a/solution.py
+++ b/solution.py
@@ -1,3 +1,5 @@
+import functools
+
 import jax
 import jax.numpy as jnp
 from jax import lax
@@ -10,9 +12,11 @@
 R = 384
 BS = 128
 CAPE = 512
-
-
-def entries_kernel(quads, count, lst, start, nxt):
+G = 4
+LEVELS = 4
+
+
+def entries_kernel(quads, count, lst, start, order, nxt):
     live = count[0]
 
     def zero(i, c):
@@ -66,6 +70,36 @@
         return c
 
     lax.fori_loop(0, live, place, 0)
+
+    def level(t):
+        return jnp.minimum((start[t + 1] - start[t] + 1) // 2, LEVELS + 1)
+
+    for k in range(LEVELS + 3):
+        nxt[k] = 0
+
+    def classes(t, c):
+        k = LEVELS + 1 - level(t)
+        nxt[k + 1] = nxt[k + 1] + 1
+        return c
+
+    lax.fori_loop(0, NP, classes, 0)
+    for k in range(LEVELS + 2):
+        nxt[k + 1] = nxt[k + 1] + nxt[k]
+
+    def pad(i, c):
+        order[i] = NP
+        return c
+
+    lax.fori_loop(0, order.shape[0], pad, 0)
+
+    def rank(t, c):
+        k = LEVELS + 1 - level(t)
+        at = nxt[k]
+        order[2 * G + at] = t
+        nxt[k] = at + 1
+        return c
+
+    lax.fori_loop(0, NP, rank, 0)
 
 
 def entries(quads, count):
@@ -75,22 +109,31 @@
         out_shape=[
             jax.ShapeDtypeStruct((CAPE + 128,), jnp.int32),
             jax.ShapeDtypeStruct((256,), jnp.int32),
+            jax.ShapeDtypeStruct((256,), jnp.int32),
         ],
         in_specs=[smem, smem],
-        out_specs=[smem, smem],
+        out_specs=[smem, smem, smem],
         scratch_shapes=[pltpu.SMEM((256,), jnp.int32)],
         cost_estimate=pl.CostEstimate(flops=10000, bytes_accessed=10000, transcendentals=0),
         name="sort_entries",
     )(quads.reshape(-1), count)
 
 
-def compute_kernel(ids, in_slot, out_slot, lst, start, core, coul, recv, factors, outbound,
-                   dens, fac, fact, half, pieces, pdt, corem, pot, acc, in_sem, fac_sem, out_sem):
+def slot_of(direct, slots, t):
+    if direct:
+        return t
+    x = t // T
+    y = lax.rem(t, T)
+    return lax.rem(x, 3) * 64 + x // 3 * 16 + y // 3 * 4 + slots[y]
+
+
+def compute_kernel(direct, ids, slots, lst, start, order, core, coul, recv, factors, outbound,
+                   dens, fac, fact, half, pieces, pdt, corem, pot, acc, cms, rhs, in_sem, fac_sem, out_sem):
     for x in range(T):
         pltpu.make_async_copy(factors.at[ids[x]], fac.at[x], fac_sem).start()
     for x in range(T):
         def fetch(y, c, x=x):
-            pltpu.make_async_copy(recv.at[in_slot[x * T + y]], dens.at[x * T + y], in_sem.at[x]).start()
+            pltpu.make_async_copy(recv.at[slot_of(direct, slots, x * T + y)], dens.at[x * T + y], in_sem.at[x]).start()
             return c
         lax.fori_loop(0, T, fetch, 0)
     corem[...] = core[...] * -0.5
@@ -125,53 +168,95 @@
     pot[...] = jnp.dot(total, core[...], precision=lax.Precision.HIGHEST, preferred_element_type=jnp.float32).reshape(NP, 1, R)
     eye = lax.broadcasted_iota(jnp.int32, (BS, BS), 0) == lax.broadcasted_iota(jnp.int32, (BS, BS), 1)
 
-    def target(t, c):
-        x = t // T
-        y = t % T
-        lo = start[t]
-        n = (start[t + 1] - lo)
-
-        def pair(k):
-            s1 = lst[lo + 2 * k]
-            s2 = jnp.where(2 * k + 1 < n, lst[lo + 2 * k + 1], NP)
-            y1 = lax.rem(s1, T)
-            y2 = lax.rem(s2, T)
-            h = jnp.concatenate([half[s1], half[s2]], axis=1)
-            w = jnp.concatenate([fact[y1], fact[y2]], axis=0)
-            return jnp.dot(h, w, preferred_element_type=jnp.float32)
-
-        acc[...] = jnp.zeros_like(acc)
-
-        def more(k, c):
-            acc[...] += pair(k)
-            return c
-
-        lax.fori_loop(0, (n + 1) // 2, more, 0)
-        row = pot[t]
-        cm = corem[...] * acc[...]
+
+    def gather_pairs(lo, n, first, pairs):
+        hs, ws = [], []
+        for k in range(2 * pairs):
+            e = first + k
+            s = jnp.where(e < n, lst[lo + e], NP)
+            hs.append(half[s])
+            ws.append(fact[lax.rem(s, T)])
+        return jnp.dot(
+            jnp.concatenate(hs, axis=1), jnp.concatenate(ws, axis=0), preferred_element_type=jnp.float32
+        )
+
+    def with_diag(cm, row):
         parts = []
         for k in range(3):
             line = cm[k * BS:(k + 1) * BS]
-            blk = line[:, k * BS:(k + 1) * BS] + jnp.where(eye, row[:, k * BS:(k + 1) * BS], 0.0)
             cols3 = [line[:, j * BS:(j + 1) * BS] for j in range(3)]
-            cols3[k] = blk
+            cols3[k] = cols3[k] + jnp.where(eye, row[:, k * BS:(k + 1) * BS], 0.0)
             parts.append(jnp.concatenate(cols3, axis=1))
-        cm = jnp.concatenate(parts, axis=0).astype(jnp.bfloat16)
-        rh = jnp.dot(cm, fac[y], preferred_element_type=jnp.float32).astype(jnp.bfloat16)
-        pieces[t] = jnp.dot(fact[x], rh, preferred_element_type=jnp.float32).astype(jnp.bfloat16)
-        pltpu.make_async_copy(pieces.at[t], outbound.at[out_slot[t]], out_sem).start()
-        return c
-
-    lax.fori_loop(0, NP, target, 0)
-    pltpu.make_async_copy(pieces, outbound.at[pl.ds(0, NP)], out_sem).wait()
-
-
-def compute(ids, in_slot, out_slot, lst, start, core, coul, recv, factors, nslots, kernel=compute_kernel):
+        return jnp.concatenate(parts, axis=0).astype(jnp.bfloat16)
+
+    def step(i, c):
+        now = lax.rem(i, 2)
+        before = 1 - now
+        tg = [order[2 * G + i * G + q] for q in range(G)]
+        t1 = [order[G + i * G + q] for q in range(G)]
+        t2 = [order[i * G + q] for q in range(G)]
+
+        def exchange(t, q, pairs, extra):
+            lo = start[t]
+            n = start[t + 1] - lo
+            if extra:
+                acc[...] = jnp.zeros_like(acc)
+
+                def more(k, c):
+                    acc[...] += gather_pairs(lo, n, 2 * k, 1)
+                    return c
+
+                lax.fori_loop(pairs, (n + 1) // 2, more, 0)
+            if pairs:
+                es = gather_pairs(lo, n, 0, pairs)
+                if extra:
+                    es = es + acc[...]
+                cm = corem[...] * es
+            else:
+                cm = jnp.zeros((R, R), jnp.float32)
+            cms[now, q] = with_diag(cm, pot[t])
+
+        def late():
+            for q in range(G):
+                x2 = jnp.minimum(t2[q], NP - 1) // T
+                pieces[t2[q]] = jnp.dot(
+                    fact[x2], rhs[now, q], preferred_element_type=jnp.float32
+                ).astype(jnp.bfloat16)
+            for q in range(G):
+                y1 = lax.rem(t1[q], T)
+                rhs[before, q] = jnp.dot(
+                    cms[before, q], fac[y1], preferred_element_type=jnp.float32
+                ).astype(jnp.bfloat16)
+
+        def branch(pairs, extra):
+            def run():
+                late()
+                for q in range(G):
+                    exchange(tg[q], q, pairs, extra)
+            return run
+
+        top = start[tg[0] + 1] - start[tg[0]]
+        top = jnp.where(i < NP // G, (top + 1) // 2, -1)
+        lax.switch(
+            jnp.minimum(top, LEVELS + 1) + 1,
+            [late] + [branch(k, False) for k in range(LEVELS + 1)] + [branch(LEVELS, True)],
+        )
+        for q in range(G):
+            @pl.when(i >= 2)
+            def _(q=q):
+                pltpu.make_async_copy(pieces.at[t2[q]], outbound.at[slot_of(direct, slots, t2[q])], out_sem).start()
+        return c
+
+    lax.fori_loop(0, NP // G + 2, step, 0)
+    pltpu.make_async_copy(pieces.at[pl.ds(0, NP)], outbound.at[pl.ds(0, NP)], out_sem).wait()
+
+
+def compute(ids, slots, lst, start, order, core, coul, recv, factors, nslots, direct=False):
     smem = pl.BlockSpec(memory_space=pltpu.SMEM)
     vmem = pl.BlockSpec(memory_space=pltpu.VMEM)
     hbm = pl.BlockSpec(memory_space=pl.ANY)
     return pl.pallas_call(
-        kernel,
+        functools.partial(compute_kernel, direct),
         out_shape=jax.ShapeDtypeStruct((nslots, BS, BS), jnp.bfloat16),
         in_specs=[smem] * 5 + [vmem] * 2 + [hbm] * 2,
         out_specs=hbm,
@@ -180,19 +265,21 @@
             pltpu.VMEM((T, R, BS), jnp.bfloat16),
             pltpu.VMEM((T, BS, R), jnp.bfloat16),
             pltpu.VMEM((NP + 1, R, BS), jnp.bfloat16),
-            pltpu.VMEM((NP, BS, BS), jnp.bfloat16),
+            pltpu.VMEM((NP + 1, BS, BS), jnp.bfloat16),
             pltpu.VMEM((R, 256), jnp.float32),
             pltpu.VMEM((R, R), jnp.float32),
             pltpu.VMEM((NP, 1, R), jnp.float32),
             pltpu.VMEM((R, R), jnp.float32),
+            pltpu.VMEM((2, G, R, R), jnp.bfloat16),
+            pltpu.VMEM((2, G, R, BS), jnp.bfloat16),
             pltpu.SemaphoreType.DMA((T,)),
             pltpu.SemaphoreType.DMA,
             pltpu.SemaphoreType.DMA,
         ],
         compiler_params=pltpu.CompilerParams(vmem_limit_bytes=50 * 2**20),
         cost_estimate=pl.CostEstimate(flops=25 * 10**9, bytes_accessed=12 * 10**6, transcendentals=0),
-        name="fock_pieces",
-    )(ids, in_slot, out_slot, lst, start, core, coul, recv, factors)
+        name="fock_pieces_direct" if direct else "fock_pieces",
+    )(ids, slots, lst, start, order, core, coul, recv, factors)
 
 
 def coulomb_table(quads, count):
@@ -204,6 +291,406 @@
     ht = (tg[:, None] == jnp.arange(NP)[None]).astype(jnp.bfloat16)
     hs = jnp.where(sr[:, None] == jnp.arange(256)[None], jnp.concatenate([live, live])[:, None] * 2.0, 0.0).astype(jnp.bfloat16)
     return lax.dot_general(ht, hs, (((0,), (0,)), ((), ())), preferred_element_type=jnp.float32)
+
+
+CAP = 10
+RELAY = 144
+MESH = pl.DeviceIdType.MESH
+ORDERS = ((2, 1, 0), (1, 0, 2), (0, 2, 1))
+
+
+def line_of(u):
+    chip = [(v * 43) >> 8 for v in u]
+    col = [v - 6 * q for v, q in zip(u, chip)]
+    e01 = chip[0] == chip[1]
+    e02 = chip[0] == chip[2]
+    e12 = chip[1] == chip[2]
+    twice = e01 | e02 | e12
+    over1 = e01
+    over2 = e02 | e12
+    where2 = jnp.where(e12, chip[1], chip[0])
+    over_col = jnp.where(e01, col[1], col[2])
+    third = jnp.where(e01, chip[2], jnp.where(e02, chip[1], chip[0]))
+    rel = (third - where2) & 3
+    return chip, col, twice, over1, over2, where2, over_col, rel
+
+
+def route_kernel(place, ids, tab, lists, idt, plus_s, minus_s, rankp_s, rankm_s):
+    z, y, x, c = place[0], place[1], place[2], place[3]
+    idt[...] = ids[...].astype(jnp.float32).T.astype(jnp.int32)
+    lane = lax.broadcasted_iota(jnp.int32, (1, 128), 1)
+    rows8 = lax.broadcasted_iota(jnp.int32, (8, 128), 0)
+    lanes8 = lax.broadcasted_iota(jnp.int32, (8, 128), 1)
+    f32 = jnp.float32
+    below = (
+        lax.broadcasted_iota(jnp.int32, (128, 128), 0) < lax.broadcasted_iota(jnp.int32, (128, 128), 1)
+    ).astype(f32).astype(jnp.bfloat16)
+
+    def prefix(m):
+        return jnp.dot(m.astype(jnp.bfloat16), below, preferred_element_type=f32)
+
+    lines = []
+    fp, fm, fl = [], [], []
+    for g in range(4):
+        u = [idt[3 * g + j:3 * g + j + 1, :] - 24 * g for j in range(3)]
+        ln = line_of(u)
+        lines.append(ln)
+        chip, col, twice, over1, over2, where2, over_col, rel = ln
+        kind = jnp.where(twice, rel, 0)
+        at = jnp.broadcast_to(where2, (8, 128)) == rows8 // 2
+        here = at & ((lanes8 & 1) == (rows8 & 1))
+        kind8 = jnp.broadcast_to(kind, (8, 128))
+        fp.append(jnp.where(here & (kind8 == 3), 1.0, 0.0))
+        fm.append(jnp.where(here & (kind8 == 1), 1.0, 0.0))
+        fl.append(jnp.where(here & (kind8 == 2), 1.0, 0.0))
+    fp = jnp.concatenate(fp, axis=0)
+    fm = jnp.concatenate(fm, axis=0)
+    fl = jnp.concatenate(fl, axis=0)
+    np_ = jnp.sum(fp, axis=1, keepdims=True)
+    nm_ = jnp.sum(fm, axis=1, keepdims=True)
+    nl_ = jnp.sum(fl, axis=1, keepdims=True)
+    give = jnp.clip(jnp.floor((nl_ + nm_ - np_ + 1.0) * 0.5), 0.0, nl_)
+    first = fl * jnp.where(prefix(fl) < give, 1.0, 0.0)
+    plus = fp + first
+    minus = fm + fl - first
+    plus_s[...] = plus
+    minus_s[...] = minus
+    rankp_s[...] = prefix(plus)
+    rankm_s[...] = prefix(minus)
+    most = jnp.max(jnp.maximum(jnp.sum(plus, axis=1, keepdims=True), jnp.sum(minus, axis=1, keepdims=True)), axis=0, keepdims=True)
+
+    me = ((z * 4 + y) * 4 + x) * 2 + c
+    own = jnp.zeros((1, 128), jnp.int32)
+    for g in range(4):
+        chip, col, twice, over1, over2, where2, over_col, rel = lines[g]
+        goes = jnp.sum(plus[8 * g:8 * g + 8], axis=0, keepdims=True) > 0.5
+        to = (where2 + jnp.where(goes, 1, 3)) & 3
+        slots = [chip[0], jnp.where(over1, to, chip[1]), jnp.where(over2, to, chip[2])]
+        for j in range(3):
+            mine = jnp.sum(jnp.where(lane == me, slots[j], 0).astype(f32), axis=1, keepdims=True)
+            own = own + jnp.where(lane == 3 * g + j, mine.astype(jnp.int32), 0)
+    own = own + jnp.where(lane == 127, (most > CAP + 0.5).astype(jnp.int32), 0)
+
+    u = [idt[pl.ds(3 * y + j, 1), :] - 24 * y for j in range(3)]
+    chip, col, twice, over1, over2, where2, over_col, rel = line_of(u)
+    rk = [idt[pl.ds(3 * z + k, 1), :] - 24 * z for k in range(3)]
+    line_row = y * 8 + x * 2 + c
+    left_row = y * 8 + ((x + 3) & 3) * 2 + c
+    right_row = y * 8 + ((x + 1) & 3) * 2 + c
+
+    def pool_col(v):
+        core = jnp.where(v >= 3, 1, 0)
+        return jnp.where(core == c, 0, 72) + v - 3 * core
+
+    main = jnp.full((1, 128), -1, jnp.int32)
+    for j, over in enumerate((chip[0] < 0, over1, over2)):
+        main = jnp.where((chip[j] == x) & jnp.logical_not(over), pool_col(col[j]), main)
+    from_left = plus_s[pl.ds(left_row, 1), :] > 0.5
+    rank_left = rankp_s[pl.ds(left_row, 1), :].astype(jnp.int32)
+    from_right = minus_s[pl.ds(right_row, 1), :] > 0.5
+    rank_right = rankm_s[pl.ds(right_row, 1), :].astype(jnp.int32)
+    for k in range(3):
+        idx = jnp.where(main >= 0, main + rk[k] * 3, -1)
+        idx = jnp.where(from_left, RELAY + rank_left, idx)
+        idx = jnp.where(from_right, RELAY + CAP + rank_right, idx)
+        tab[k:k + 1, :] = idx
+    tab[3:7, :] = jnp.zeros((4, 128), jnp.int32)
+    tab[7:8, :] = own
+
+    j16 = lax.broadcasted_iota(jnp.int32, (16, 128), 0)
+    l16 = lax.broadcasted_iota(jnp.int32, (16, 128), 1)
+    out = jnp.zeros((16, 128), jnp.int32)
+
+    def listed(flag, rank, value):
+        sel = jnp.broadcast_to(flag, (16, 128)) & (jnp.broadcast_to(rank, (16, 128)) == j16)
+        got = jnp.sum(jnp.where(sel, jnp.broadcast_to(value, (16, 128)) + 1, 0).astype(f32), axis=1, keepdims=True)
+        return got.astype(jnp.int32) - 1
+
+    my_plus = plus_s[pl.ds(line_row, 1), :] > 0.5
+    my_rankp = rankp_s[pl.ds(line_row, 1), :].astype(jnp.int32)
+    my_minus = minus_s[pl.ds(line_row, 1), :] > 0.5
+    my_rankm = rankm_s[pl.ds(line_row, 1), :].astype(jnp.int32)
+    for k in range(3):
+        value = pool_col(over_col) + rk[k] * 3
+        out = jnp.where(l16 == k, listed(my_plus, my_rankp, value), out)
+        out = jnp.where(l16 == 3 + k, listed(my_minus, my_rankm, value), out)
+    out = jnp.where(l16 == 6, listed(from_left, rank_left, lane), out)
+    out = jnp.where(l16 == 7, listed(from_right, rank_right, lane), out)
+    lists[...] = out
+
+
+def route(place, ids):
+    smem = pl.BlockSpec(memory_space=pltpu.SMEM)
+    vmem = pl.BlockSpec(memory_space=pltpu.VMEM)
+    return pl.pallas_call(
+        route_kernel,
+        out_shape=[jax.ShapeDtypeStruct((8, 128), jnp.int32), jax.ShapeDtypeStruct((16, 128), jnp.int32)],
+        in_specs=[smem, vmem],
+        out_specs=[vmem, vmem],
+        scratch_shapes=[pltpu.VMEM((128, 128), jnp.int32)] + [pltpu.VMEM((32, 128), jnp.float32)] * 4,
+        name="route_tasks",
+    )(place, ids)
+
+
+def here():
+    z = lax.axis_index("row")
+    b = lax.axis_index("bulk")
+    return b // 2 % 4, b // 8, z, b % 2
+
+
+def device(x, y, z, c):
+    return (z, y * 8 + x * 2 + c)
+
+
+def moved(at, axis, by):
+    pos = list(at[:3])
+    pos[axis] = lax.rem(pos[axis] + by, 4)
+    return device(*pos, at[3])
+
+
+def greet(at):
+    barrier = pltpu.get_barrier_semaphore()
+    for axis in range(3):
+        for by in (1, 2, 3):
+            pl.semaphore_signal(barrier, inc=1, device_id=moved(at, axis, by), device_id_type=MESH)
+    pl.semaphore_wait(barrier, 9)
+
+
+def part(ref, axis, index):
+    if axis == 2:
+        return ref.at[index]
+    if axis == 1:
+        return ref.at[:, index]
+    return ref.at[:, :, index]
+
+
+def phase_copies(at, k, step, src, dst, send, recv, local):
+    axis = ORDERS[k][step]
+    own = at[axis]
+    copies = [pltpu.make_async_copy(part(src, axis, own), part(dst, axis, own), local.at[k, step])]
+    for by in (1, 2, 3):
+        to = lax.rem(own + by, 4)
+        copies.append(
+            pltpu.make_async_remote_copy(
+                part(src, axis, to), part(dst, axis, own),
+                send.at[k, step, by - 1], recv.at[k, step, by - 1],
+                device_id=moved(at, axis, by), device_id_type=MESH,
+            )
+        )
+    return copies
+
+
+def start_all(copies):
+    for copy in copies:
+        copy.start()
+
+
+def wait_all(copies):
+    for copy in copies:
+        copy.wait()
+
+
+def fetch_kernel(tab, lists, density, sibling, out, pool, r0, r1, r2, rs, a, b, d,
+                 load, relay_send, relay_recv, send, recv, local):
+    at = here()
+    c = at[3]
+    mine = pltpu.make_async_copy(density, pool.at[pl.ds(0, 72)], load.at[0])
+    other = pltpu.make_async_copy(sibling, pool.at[pl.ds(72, 72)], load.at[1])
+    mine.start()
+    other.start()
+    greet(at)
+    mine.wait()
+    other.wait()
+    relayed = (r0, r1, r2)
+    relays = []
+    for k in range(3):
+        def fill(j, cc, k=k):
+            rs[k, j] = pool[jnp.maximum(lists[j, k], 0)]
+            rs[k, CAP + j] = pool[jnp.maximum(lists[j, 3 + k], 0)]
+            return cc
+        lax.fori_loop(0, CAP, fill, 0)
+        pair = [
+            pltpu.make_async_remote_copy(
+                rs.at[k, pl.ds(CAP * side, CAP)], relayed[k].at[pl.ds(CAP * side, CAP)],
+                relay_send.at[k, side], relay_recv.at[k, side],
+                device_id=moved(at, 0, 1 if side == 0 else 3), device_id_type=MESH,
+            )
+            for side in range(2)
+        ]
+        start_all(pair)
+        relays.append(pair)
+    steps = []
+    for k in range(3):
+        wait_all(relays[k])
+
+        def fill(i, cc, k=k):
+            index = tab[k, 2 * i + c]
+            plain = pool[jnp.clip(index, 0, 143)]
+            passed = relayed[k][jnp.maximum(index - RELAY, 0)]
+            a[k, i // 16, i // 4 % 4, i % 4] = jnp.where(index >= RELAY, passed, plain)
+            return cc
+
+        lax.fori_loop(0, 64, fill, 0)
+        copies = phase_copies(at, k, 0, a.at[k], b.at[k], send, recv, local)
+        start_all(copies)
+        steps.append(copies)
+    for step, src, dst in ((1, b, d), (2, d, out)):
+        for k in range(3):
+            wait_all(steps[k])
+            copies = phase_copies(at, k, step, src.at[k], dst.at[k], send, recv, local)
+            start_all(copies)
+            steps[k] = copies
+    for k in range(3):
+        wait_all(steps[k])
+
+
+def fetch_blocks(tab, lists, density, sibling):
+    smem = pl.BlockSpec(memory_space=pltpu.SMEM)
+    hbm = pl.BlockSpec(memory_space=pl.ANY)
+    cube = pltpu.VMEM((3, 4, 4, 4, BS, BS), jnp.bfloat16)
+    dma = pltpu.SemaphoreType.DMA
+    return pl.pallas_call(
+        fetch_kernel,
+        out_shape=jax.ShapeDtypeStruct((3, 4, 4, 4, BS, BS), jnp.bfloat16),
+        in_specs=[smem, smem, hbm, hbm],
+        out_specs=hbm,
+        scratch_shapes=[pltpu.VMEM((144, BS, BS), jnp.bfloat16)]
+        + [pltpu.VMEM((2 * CAP, BS, BS), jnp.bfloat16)] * 3
+        + [pltpu.VMEM((3, 2 * CAP, BS, BS), jnp.bfloat16), cube, cube, cube]
+        + [dma((2,)), dma((3, 2)), dma((3, 2)), dma((3, 3, 3)), dma((3, 3, 3)), dma((3, 3))],
+        compiler_params=pltpu.CompilerParams(
+            collective_id=1, has_side_effects=True, vmem_limit_bytes=50 * 2**20
+        ),
+        name="fetch_blocks",
+    )(tab, lists, density.reshape(72, BS, BS), sibling.reshape(72, BS, BS))
+
+
+def return_kernel(lists, pieces, out, back, b, d, e0, e1, e2, rs,
+                  relay_send, relay_recv, send, recv, local, store):
+    at = here()
+    greet(at)
+    ends = (e0, e1, e2)
+    steps = []
+    for k in range(3):
+        copies = phase_copies(at, k, 0, pieces.at[k], b.at[k], send, recv, local)
+        start_all(copies)
+        steps.append(copies)
+    for k in range(3):
+        wait_all(steps[k])
+        steps[k] = phase_copies(at, k, 1, b.at[k], d.at[k], send, recv, local)
+        start_all(steps[k])
+    for k in range(3):
+        wait_all(steps[k])
+        steps[k] = phase_copies(at, k, 2, d.at[k], ends[k], send, recv, local)
+        start_all(steps[k])
+    for k in range(3):
+        wait_all(steps[k])
+        kept = pltpu.make_async_copy(ends[k], out.at[k], store.at[k])
+        kept.start()
+
+        def fill(j, cc, k=k):
+            for side in range(2):
+                t = jnp.maximum(lists[j, 6 + side], 0) // 2
+                rs[k, side * CAP + j] = ends[k][t // 16, t // 4 % 4, t % 4]
+            return cc
+
+        lax.fori_loop(0, CAP, fill, 0)
+        pair = [
+            pltpu.make_async_remote_copy(
+                rs.at[k, pl.ds(CAP * side, CAP)], back.at[k, pl.ds(CAP * side, CAP)],
+                relay_send.at[k, side], relay_recv.at[k, side],
+                device_id=moved(at, 0, 3 if side == 0 else 1), device_id_type=MESH,
+            )
+            for side in range(2)
+        ]
+        start_all(pair)
+        steps[k] = pair + [kept]
+    for k in range(3):
+        wait_all(steps[k])
+
+
+def return_pieces(lists, pieces):
+    smem = pl.BlockSpec(memory_space=pltpu.SMEM)
+    hbm = pl.BlockSpec(memory_space=pl.ANY)
+    cube = pltpu.VMEM((3, 4, 4, 4, BS, BS), jnp.bfloat16)
+    dma = pltpu.SemaphoreType.DMA
+    return pl.pallas_call(
+        return_kernel,
+        out_shape=[
+            jax.ShapeDtypeStruct((3, 4, 4, 4, BS, BS), jnp.bfloat16),
+            jax.ShapeDtypeStruct((3, 2 * CAP, BS, BS), jnp.bfloat16),
+        ],
+        in_specs=[smem, hbm],
+        out_specs=[hbm, hbm],
+        scratch_shapes=[cube, cube]
+        + [pltpu.VMEM((4, 4, 4, BS, BS), jnp.bfloat16)] * 3
+        + [pltpu.VMEM((3, 2 * CAP, BS, BS), jnp.bfloat16)]
+        + [dma((3, 2)), dma((3, 2)), dma((3, 3, 3)), dma((3, 3, 3)), dma((3, 3)), dma((3,))],
+        compiler_params=pltpu.CompilerParams(
+            collective_id=2, has_side_effects=True, vmem_limit_bytes=50 * 2**20
+        ),
+        name="return_pieces",
+    )(lists, pieces)
+
+
+def collect_kernel(place, tab, lists, got, back, own, other, acc):
+    c = place[3]
+    acc[...] = jnp.zeros_like(acc)
+    own[...] = jnp.zeros_like(own)
+
+    def put(index, block):
+        @pl.when((index >= 0) & (index < 72))
+        def _():
+            own[jnp.clip(index, 0, 71)] += block().astype(jnp.float32)
+
+        @pl.when((index >= 72) & (index < 144))
+        def _():
+            acc[jnp.clip(index - 72, 0, 71)] += block().astype(jnp.float32)
+
+    def add(i, cc):
+        for k in range(3):
+            put(tab[k, 2 * i + c], lambda: got[k, i])
+        return cc
+
+    lax.fori_loop(0, 64, add, 0)
+
+    def add_back(j, cc):
+        for k in range(3):
+            for side in range(2):
+                put(lists[j, 3 * side + k], lambda: back[k, side * CAP + j])
+        return cc
+
+    lax.fori_loop(0, CAP, add_back, 0)
+    other[...] = acc[...].astype(jnp.bfloat16)
+
+
+def collect(place, tab, lists, got, back):
+    smem = pl.BlockSpec(memory_space=pltpu.SMEM)
+    vmem = pl.BlockSpec(memory_space=pltpu.VMEM)
+    return pl.pallas_call(
+        collect_kernel,
+        out_shape=[
+            jax.ShapeDtypeStruct((72, BS, BS), jnp.float32),
+            jax.ShapeDtypeStruct((72, BS, BS), jnp.bfloat16),
+        ],
+        in_specs=[smem, smem, smem, vmem, vmem],
+        out_specs=[vmem, vmem],
+        scratch_shapes=[pltpu.VMEM((72, BS, BS), jnp.float32)],
+        compiler_params=pltpu.CompilerParams(vmem_limit_bytes=50 * 2**20),
+        name="collect_pieces",
+    )(place, tab, lists, got.reshape(3, 64, BS, BS), back)
+
+
+def swap_cores(value):
+    return lax.ppermute(value, "bulk", [(i, i ^ 1) for i in range(32)])
+
+
+def fast_path(density, factors, core, mine, sibling, tables, place, tab, lists, coul):
+    recv = fetch_blocks(tab, lists, density, sibling).reshape(192, BS, BS)
+    pieces = compute(mine, tab[7], *tables, core, coul, recv, factors, 192)
+    got, back = return_pieces(lists, pieces.reshape(3, 4, 4, 4, BS, BS))
+    own, other = collect(place, tab, lists, got, back)
+    return (own + swap_cores(other).astype(jnp.float32)).reshape(24, 3, BS, BS)
 
 
 def column_of(ids, d, bulk):
@@ -299,22 +786,37 @@
     )(place, ids, inbound)
 
 
+def slow_path(density, factors, core, mine, tables, place, ids, coul):
+    axes = ("row", "bulk")
+    where = jnp.stack([place[0], place[1] * 8 + place[2] * 2 + place[3]])
+    ids = ids[:, :T].reshape(-1)
+    sent = pack(where, ids, density)
+    recv = lax.all_to_all(sent, axes, split_axis=0, concat_axis=0, tiled=True)
+    owner = mine[:, None] // 24 * 32 + mine[None, :] // 3
+    slot = (owner * 3 + (jnp.arange(T) % 3)[:, None]).reshape(-1)
+    pieces = compute(mine, mine, *tables, core, coul, recv[slot], factors, NP, direct=True)
+    outbound = jnp.zeros((384, BS, BS), jnp.bfloat16).at[slot].set(pieces)
+    inbound = lax.all_to_all(outbound, axes, split_axis=0, concat_axis=0, tiled=True)
+    return gather(where, ids, inbound)
+
+
 def shards(density, factors, core, task_blocks, quartets, quartet_count):
     axes = ("row", "bulk")
     mine = task_blocks[0]
-    place = jnp.stack([lax.axis_index("row"), lax.axis_index("bulk")]).astype(jnp.int32)
+    bulk = lax.axis_index("bulk")
+    place = jnp.stack([lax.axis_index("row"), bulk // 8, bulk // 2 % 4, bulk % 2]).astype(jnp.int32)
     ids = lax.all_to_all(
-        jnp.broadcast_to(mine[None], (128, T)), axes, split_axis=0, concat_axis=0, tiled=True
-    ).reshape(-1)
-    sent = pack(place, ids, density)
-    recv = lax.all_to_all(sent, axes, split_axis=0, concat_axis=0, tiled=True)
-    lst, start = entries(quartets, quartet_count)
+        jnp.broadcast_to(jnp.pad(mine, (0, 116))[None], (128, 128)), axes, split_axis=0, concat_axis=0, tiled=True
+    )
+    sibling = swap_cores(density)
+    tables = entries(quartets, quartet_count)
     coul = coulomb_table(quartets, quartet_count[0])
-    owner = mine[:, None] // 24 * 32 + mine[None, :] // 3
-    slot = (owner * 3 + (jnp.arange(T) % 3)[:, None]).reshape(-1).astype(jnp.int32)
-    outbound = compute(mine, slot, slot, lst, start, core, coul, recv, factors, 384)
-    inbound = lax.all_to_all(outbound, axes, split_axis=0, concat_axis=0, tiled=True)
-    return gather(place, ids, inbound)
+    tab, lists = route(place, ids)
+    return lax.cond(
+        tab[7, 127] > 0,
+        lambda: slow_path(density, factors, core, mine, tables, place, ids, coul),
+        lambda: fast_path(density, factors, core, mine, sibling, tables, place, tab, lists, coul),
+    )
 
 
 def solution(mesh):

time: 711 us -> 358 us (0.50)
  blocking collectives: 238 us -> 0 us
  waiting for transfers between devices: 151 us -> 4.38 us
  Pallas kernels: 274 us -> 313 us
  starting transfers between devices: 39.8 us -> 12.7 us
  loops' own time: 0 us -> 10.1 us
    all_to_all x1 -> x0, blocking collectives: 238 us -> none  [shards(): lax.all_to_all(outbound, axes, split_axis=0, concat_axis=0, tiled=True)]
    all_to_all x2 -> x1, waiting for transfers between devices: 151 us -> 0.01 us  [shards(): lax.all_to_all(jnp.broadcast_to(jnp.pad(mine, (0, 116))[None], (128, 128)...]
    all_to_all x2 -> x1, starting transfers between devices: 39.8 us -> 10.2 us  [shards(): lax.all_to_all(jnp.broadcast_to(jnp.pad(mine, (0, 116))[None], (128, 128)...]
    pallas_call x3 -> x5, Pallas kernels: 267 us -> 295 us  [the longest x1 107 us: return_pieces(): pl.pallas_call(return_kernel, out_shape=[jax.ShapeDtypeStruct((3, 4, 4, 4...]
    pallas_call x1, Pallas kernels: 7.27 us -> 17.8 us  [entries(): pl.pallas_call(entries_kernel, out_shape=[jax.ShapeDtypeStruct((CAPE + 12...]
    another operation x0 -> x1, loops' own time: none -> 10.1 us  [shards(): lax.cond(tab[7, 127] > 0, lambda: slow_path(density, factors, core, mine,...]
  transfers between devices with their start and end apart: 2 -> 3, of which waited for: 2 -> 1; matrix products, arithmetic and copies ran while one was open for 0% -> 1% of each run, Pallas kernels for 1% -> 5%
where the time goes in v2:
time: 358 us; the launch traced here: 353 us
  Pallas kernels  313 us (87%)
  starting transfers between devices  12.7 us (4%)
  loops' own time  10.1 us (3%)
  other arithmetic  6.53 us (2%)
  waiting for transfers between devices  4.38 us (1%)
    pallas_call x1, Pallas kernels, return_pieces(): pl.pallas_call(return_kernel, out_shape=[jax.ShapeDtypeStruct((3, 4, 4, 4...  107 us
    pallas_call x1, Pallas kernels, fetch_blocks(): pl.pallas_call(fetch_kernel, out_shape=jax.ShapeDtypeStruct((3, 4, 4, 4,...  104 us
    pallas_call x1, Pallas kernels, compute(): pl.pallas_call(functools.partial(compute_kernel, direct), out_shape=jax.S...  71.4 us
    pallas_call x1, Pallas kernels, entries(): pl.pallas_call(entries_kernel, out_shape=[jax.ShapeDtypeStruct((CAPE + 12...  17.8 us
    pallas_call x1, Pallas kernels, collect(): pl.pallas_call(collect_kernel, out_shape=[jax.ShapeDtypeStruct((72, BS, B...  11.9 us
    all_to_all x1, starting transfers between devices, shards(): lax.all_to_all(jnp.broadcast_to(jnp.pad(mine, (0, 116))[None], (128, 128)...  10.2 us
    another operation x1, loops' own time, shards(): lax.cond(tab[7, 127] > 0, lambda: slow_path(density, factors, core, mine,...  10.1 us
  transfers between devices with their start and end apart: 3, of which 1 were waited for; matrix products, arithmetic and copies ran while one was open for 1% of the time, Pallas kernels for 5%

profile of v2, /device:TPU:1, one launch (start us, length us, event | category | flops | bytes accessed | tf_op | source)
XLA Modules:
  0.0 353.2 jit_solution(15331777342649444534)
XLA Ops:
  0.0 1.4 collective-permute-start.1
  2.1 0.8 copy.10
  2.9 0.7 reshape.154.quads
  3.6 0.7 pad.4
  4.2 0.7 broadcast_in_dim.10
  4.9 10.2 %all-to-all-start.2 = ((s32[128,1,128]{2,1,0:T(1,128)}), s32[128,1,128]{2,1,0:T(1,128)S(1)}, u32[]{:S(2)}, u32[]{:S(2)}) async-start(s32[128,1,128]{2,1,0:T(1,128)} %broadcast_in_dim.10), calls=%async_computation.2 | async-start | bytes 131072 | tf_op jit(solution)/shard_map/all_to_all | solution.py:808
  15.1 17.8 %sort_entries.1 = (s32[640]{0:T(1024)S(1)}, s32[256]{0:T(256)S(1)}, s32[256]{0:T(256)S(1)}) custom-call(s32[512]{0:T(512)} %reshape.154.quads, s32[1]{0:T(128)} %copy.14.count), custom_call_target="tpu_custom_call" | custom-call | flops 10000 | bytes 10000 | tf_op jit(solution)/shard_map/sort_entries/pallas_call | solution.py:107
  33.0 0.8 add_bitcast_fusion
  33.8 0.3 fusion.2
  34.2 0.1 pad_add_fusion.3.place
  34.3 0.0 all-to-all-done.2
  34.3 1.0 route_tasks.1
  35.3 0.6 slice.21
  36.5 0.0 collective-permute-done.1
  36.5 315.6 %conditional.1 = (f32[24,3,128,128]{3,2,1,0:T(8,128)}) conditional(s32[]{:T(128)} %bitcast.18, (s32[8,128]{1,0:T(8,128)S(1)}, bf16[24,3,128,128]{3,2,1,0:T(8,128)(2,1)}, bf16[24,3,128,128]{3,2,1,0:T(8,128)(2,1)S(1)}, s32[16,128]{1,0:T(8,128)S(1)}, s32[12]{0:T(128)}, /*index=5*/s32[640]{0:T(1024)S(1)}, s32[256]{0:T(256)S(1)}, s32[256]{0:T(256)S(1)}, ...), branch_computations={%region_0.1_spmd, %region_1.3_spmd} | conditional | flops 25002358784 | bytes 113496120 | solution.py:815
  36.5 0.0 copy-start.2
  36.5 0.0 copy-start.3
  36.6 0.0 copy-start.5
  36.6 103.9 %fetch_blocks.1 = bf16[3,4,4,4,128,128]{5,4,3,2,1,0:T(8,128)(2,1)} custom-call(s32[8,128]{1,0:T(8,128)S(1)} %get-tuple-element.61.tab, s32[16,128]{1,0:T(8,128)S(1)} %get-tuple-element.62.lists, bf16[72,128,128]{2,1,0:T(8,128)(2,1)} %bitcast.35, bf16[72,128,128]{2,1,0:T(8,128)(2,1)S(1)} %bitcast.39), custom_call_target="tpu_custom_call" | custom-call | tf_op jit(solution)/shard_map/cond/branch_0_fun/fetch_blocks/pallas_call | solution.py:552
  140.5 0.0 copy-done.2
  140.5 0.0 copy-done.3
  140.5 0.0 copy-done.5
  140.5 71.4 %fock_pieces.1 = bf16[192,128,128]{2,1,0:T(8,128)(2,1)} custom-call(s32[12]{0:T(128)S(1)} %copy-done.5, s32[128]{0:T(128)S(1)} %slice_bitcast_fusion.slots, s32[640]{0:T(1024)S(1)} %get-tuple-element.64.lst, s32[256]{0:T(256)S(1)} %get-tuple-element.65.start, s32[256]{0:T(256)S(1)} %get-tuple-element.66.order, f32[384,384]{1,0:T(8,128)S(1)} %copy-done.3, ...), custom_call_target="tpu_custom_call" | custom-call | flops 24999999488 | bytes 12000000 | tf_op jit(solution)/shard_map/cond/branch_0_fun/fock_pieces/pallas_call | solution.py:258
  211.9 107.2 %return_pieces.1 = (bf16[3,4,4,4,128,128]{5,4,3,2,1,0:T(8,128)(2,1)}, bf16[3,20,128,128]{3,2,1,0:T(8,128)(2,1)S(1)}) custom-call(s32[16,128]{1,0:T(8,128)S(1)} %get-tuple-element.62.lists, bf16[3,4,4,4,128,128]{5,4,3,2,1,0:T(8,128)(2,1)} %bitcast.37), custom_call_target="tpu_custom_call" | custom-call | tf_op jit(solution)/shard_map/cond/branch_0_fun/return_pieces/pallas_call | solution.py:617
  319.1 11.9 %collect_pieces.1 = (f32[72,128,128]{2,1,0:T(8,128)}, bf16[72,128,128]{2,1,0:T(8,128)(2,1)}) custom-call(s32[4]{0:T(128)S(1)} %get-tuple-element.60.place, s32[8,128]{1,0:T(8,128)S(1)} %get-tuple-element.61.tab, s32[16,128]{1,0:T(8,128)S(1)} %get-tuple-element.62.lists, bf16[3,64,128,128]{3,2,1,0:T(8,128)(2,1)} %bitcast.36, ...), custom_call_target="tpu_custom_call" | custom-call | tf_op jit(solution)/shard_map/cond/branch_0_fun/collect_pieces/pallas_call | solution.py:670
  331.1 1.1 collective-permute-start
  332.1 4.4 %collective-permute-done = bf16[72,128,128]{2,1,0:T(8,128)(2,1)S(1)} collective-permute-done((bf16[72,128,128]{2,1,0:T(8,128)(2,1)}, bf16[72,128,128]{2,1,0:T(8,128)(2,1)S(1)}, u32[]{:S(2)}, u32[]{:S(2)}) %collective-permute-start) | collective-permute-done | bytes 2359328 | tf_op jit(solution)/shard_map/cond/branch_0_fun/ppermute | solution.py:685
  336.5 5.6 %convert_add_fusion = f32[72,128,128]{2,1,0:T(8,128)} fusion(f32[72,128,128]{2,1,0:T(8,128)} %get-tuple-element.74, bf16[72,128,128]{2,1,0:T(8,128)(2,1)S(1)} %collective-permute-done), kind=kLoop, calls=%fused_computation.2 | loop fusion | flops 2359296 | bytes 11796480 | tf_op jit(solution)/shard_map/cond/branch_0_fun/add | solution.py:693
  (4 shorter events, 0.0 us)
Async XLA Ops:
  0.0 36.5 %collective-permute-start.1 = (bf16[24,3,128,128]{3,2,1,0:T(8,128)(2,1)}, bf16[24,3,128,128]{3,2,1,0:T(8,128)(2,1)S(1)}, u32[]{:S(2)}, u32[]{:S(2)}) collective-permute-start(bf16[24,3,128,128]{3,2,1,0:T(8,128)(2,1)} %param.8), channel_id=1, source_target_pairs={{0,1},{1,0},{2,3},{3,2},{4,5},{5,4},{6,7},{7,6},{8,9},{9,8},{10,11... | collective-permute-start | bytes 7077896 | tf_op jit(solution)/shard_map/ppermute | solution.py:685
  4.9 29.4 %all-to-all-start.2 = ((s32[128,1,128]{2,1,0:T(1,128)}), s32[128,1,128]{2,1,0:T(1,128)S(1)}, u32[]{:S(2)}, u32[]{:S(2)}) async-start(s32[128,1,128]{2,1,0:T(1,128)} %broadcast_in_dim.10), calls=%async_computation.2 | async-start | bytes 131072 | tf_op jit(solution)/shard_map/all_to_all | solution.py:808
  36.5 103.9 %copy-start.2 = (bf16[96,384,128]{2,1,0:T(8,128)(2,1)S(1)}, bf16[96,384,128]{2,1,0:T(8,128)(2,1)}, u32[]{:S(2)}) copy-start(bf16[96,384,128]{2,1,0:T(8,128)(2,1)} %get-tuple-element.71.factors) | copy-start | bytes 28311556 | tf_op jit(solution)/shard_map/cond
  36.5 103.9 %copy-start.3 = (f32[384,384]{1,0:T(8,128)S(1)}, f32[384,384]{1,0:T(8,128)}, u32[]{:S(2)}) copy-start(f32[384,384]{1,0:T(8,128)} %get-tuple-element.67.core) | copy-start | bytes 1769476 | tf_op jit(solution)/shard_map/cond
  36.6 103.9 %copy-start.5 = (s32[12]{0:T(128)S(1)}, s32[12]{0:T(128)}, u32[]{:S(2)}) copy-start(s32[12]{0:T(128)} %get-tuple-element.63.ids) | copy-start | bytes 148 | tf_op jit(solution)/shard_map/cond
  331.1 5.4 %collective-permute-start = (bf16[72,128,128]{2,1,0:T(8,128)(2,1)}, bf16[72,128,128]{2,1,0:T(8,128)(2,1)S(1)}, u32[]{:S(2)}, u32[]{:S(2)}) collective-permute-start(bf16[72,128,128]{2,1,0:T(8,128)(2,1)} %get-tuple-element.75), channel_id=1, source_target_pairs={{0,1},{1,0},{2,3},{3,2},{4,5},{5,4},{6,7},{7,6},{8,9},{9,8},{10,11... | collective-permute-start | bytes 7077896 | tf_op jit(solution)/shard_map/cond/branch_0_fun/ppermute | solution.py:685

commit v3 on v2

--- a/solution.py
+++ b/solution.py
@@ -13,122 +13,92 @@
 BS = 128
 CAPE = 512
 G = 4
-LEVELS = 4
-
-
-def entries_kernel(quads, count, lst, start, order, nxt):
-    live = count[0]
-
-    def zero(i, c):
-        start[i] = 0
-        return c
-
-    lax.fori_loop(0, NP + 1, zero, 0)
-
-    def quad(i):
-        return quads[4 * i], quads[4 * i + 1], quads[4 * i + 2], quads[4 * i + 3]
-
-    def add(t):
-        start[t + 1] = start[t + 1] + 1
-
-    def tally(i, c):
-        a, b, d, e = quad(i)
-        add(a * T + d)
-        add(a * T + e)
-        add(b * T + d)
-        add(b * T + e)
-        return c
-
-    lax.fori_loop(0, live, tally, 0)
-
-    def running(i, total):
-        total = total + start[i + 1]
-        start[i + 1] = total
-        nxt[i + 1] = total
-        return total
-
-    nxt[0] = 0
-    lax.fori_loop(0, NP, running, 0)
-
-    def fill(i, c):
-        lst[i] = NP
-        return c
-
-    lax.fori_loop(0, lst.shape[0], fill, 0)
-
-    def put(t, s):
-        at = nxt[t]
-        lst[at] = s
-        nxt[t] = at + 1
-
-    def place(i, c):
-        a, b, d, e = quad(i)
-        put(a * T + d, b * T + e)
-        put(a * T + e, b * T + d)
-        put(b * T + d, a * T + e)
-        put(b * T + e, a * T + d)
-        return c
-
-    lax.fori_loop(0, live, place, 0)
-
-    def level(t):
-        return jnp.minimum((start[t + 1] - start[t] + 1) // 2, LEVELS + 1)
-
-    for k in range(LEVELS + 3):
-        nxt[k] = 0
-
-    def classes(t, c):
-        k = LEVELS + 1 - level(t)
-        nxt[k + 1] = nxt[k + 1] + 1
-        return c
-
-    lax.fori_loop(0, NP, classes, 0)
-    for k in range(LEVELS + 2):
-        nxt[k + 1] = nxt[k + 1] + nxt[k]
-
-    def pad(i, c):
-        order[i] = NP
-        return c
-
-    lax.fori_loop(0, order.shape[0], pad, 0)
-
-    def rank(t, c):
-        k = LEVELS + 1 - level(t)
-        at = nxt[k]
-        order[2 * G + at] = t
-        nxt[k] = at + 1
-        return c
-
-    lax.fori_loop(0, NP, rank, 0)
+LEVELS = 7
+STRIP = 64
+
+
+def entries_kernel(quads, count, tables, coul):
+    f32 = jnp.float32
+    live = lax.broadcasted_iota(jnp.int32, (128, 1), 0) < count[0]
+    q = quads[...]
+    a, b, c, e = (q[:, n:n + 1] for n in range(4))
+    lanes = lax.broadcasted_iota(jnp.int32, (128, 256), 1)
+
+    def hot(t):
+        return jnp.where((t == lanes) & live, 1.0, 0.0)
+
+    def product(u, v):
+        return jnp.dot(u.T.astype(jnp.bfloat16), v.astype(jnp.bfloat16), preferred_element_type=f32)
+
+    bra = hot(a * T + b)
+    ket = hot(c * T + e)
+    table = 2.0 * (product(bra, ket) + product(ket, bra))
+    coul[...] = table[:NP, :NP]
+
+    targets = [a * T + c, a * T + e, b * T + c, b * T + e]
+    sources = [b * T + e, b * T + c, a * T + e, a * T + c]
+    member = jnp.concatenate([hot(t) for t in targets], axis=0)
+    source = jnp.concatenate(sources, axis=0).astype(f32)
+    older = lax.broadcasted_iota(jnp.int32, (CAPE, CAPE), 0) > lax.broadcasted_iota(jnp.int32, (CAPE, CAPE), 1)
+    rank = jnp.dot(
+        jnp.where(older, 1.0, 0.0).astype(jnp.bfloat16), member.astype(jnp.bfloat16), preferred_element_type=f32
+    )
+    counts = jnp.broadcast_to(jnp.sum(member, axis=0, keepdims=True), (8, 256))
+    row = lax.broadcasted_iota(jnp.int32, (256, 256), 0)
+    col = lax.broadcasted_iota(jnp.int32, (256, 256), 1)
+    start = jnp.dot(
+        counts, jnp.where(row < col, 1.0, 0.0), precision=lax.Precision.HIGHEST, preferred_element_type=f32
+    )
+    used = jnp.sum(member, axis=1, keepdims=True) > 0.5
+    place = jnp.sum(member * (rank + start[0:1]), axis=1, keepdims=True)
+    place = jnp.where(used, place, -1.0).astype(jnp.int32)
+    spots = lax.broadcasted_iota(jnp.int32, (CAPE, CAPE + 128), 1)
+    filled = jnp.sum(jnp.where(place == spots, source - NP, 0.0), axis=0, keepdims=True)
+
+    level = jnp.minimum(counts, LEVELS + 1.0)
+    level = jnp.where(lax.broadcasted_iota(jnp.int32, (8, 256), 1) < NP, level, -1.0)
+    across = jnp.broadcast_to(level[0:1], (256, 256))
+    down = across.T
+    ahead = (across > down) | ((across == down) & (col < row))
+    spot = jnp.sum(jnp.where(ahead, 1.0, 0.0), axis=1, keepdims=True).astype(jnp.int32)
+    order = jnp.sum(jnp.where(spot == col, row, 0).astype(f32), axis=0, keepdims=True)
+    order = jnp.minimum(order, float(NP))
+    tables[0:1, :] = (filled + NP).astype(jnp.int32)
+    tables[1:2, 0:256] = start[0:1].astype(jnp.int32)
+    tables[2:3, 0:256] = order.astype(jnp.int32)
 
 
 def entries(quads, count):
     smem = pl.BlockSpec(memory_space=pltpu.SMEM)
+    vmem = pl.BlockSpec(memory_space=pltpu.VMEM)
     return pl.pallas_call(
         entries_kernel,
         out_shape=[
-            jax.ShapeDtypeStruct((CAPE + 128,), jnp.int32),
-            jax.ShapeDtypeStruct((256,), jnp.int32),
-            jax.ShapeDtypeStruct((256,), jnp.int32),
+            jax.ShapeDtypeStruct((8, CAPE + 128), jnp.int32),
+            jax.ShapeDtypeStruct((NP, NP), jnp.float32),
         ],
-        in_specs=[smem, smem],
-        out_specs=[smem, smem, smem],
-        scratch_shapes=[pltpu.SMEM((256,), jnp.int32)],
+        in_specs=[vmem, smem],
+        out_specs=[vmem, vmem],
         cost_estimate=pl.CostEstimate(flops=10000, bytes_accessed=10000, transcendentals=0),
         name="sort_entries",
-    )(quads.reshape(-1), count)
+    )(quads, count)
+
+
+def split(t):
+    x = (t * 171) >> 11
+    return x, t - x * T
 
 
 def slot_of(direct, slots, t):
     if direct:
         return t
-    x = t // T
-    y = lax.rem(t, T)
-    return lax.rem(x, 3) * 64 + x // 3 * 16 + y // 3 * 4 + slots[y]
-
-
-def compute_kernel(direct, ids, slots, lst, start, order, core, coul, recv, factors, outbound,
-                   dens, fac, fact, half, pieces, pdt, corem, pot, acc, cms, rhs, in_sem, fac_sem, out_sem):
+    x, y = split(t)
+    z = (x * 11) >> 5
+    return (x - 3 * z) * 64 + z * 16 + ((y * 11) >> 5) * 4 + slots[y]
+
+
+def compute_kernel(direct, ids, slots, tables, core, coul, recv, factors, outbound,
+                   dens, fac, fact, pw, ha, hb, corem, pot, cma, cmb, rha, rhb, in_sem, fac_sem, out_sem):
     for x in range(T):
         pltpu.make_async_copy(factors.at[ids[x]], fac.at[x], fac_sem).start()
     for x in range(T):
@@ -137,163 +107,164 @@
             return c
         lax.fori_loop(0, T, fetch, 0)
     corem[...] = core[...] * -0.5
-    half[NP] = jnp.zeros((R, BS), jnp.bfloat16)
-    pdt[...] = jnp.zeros_like(pdt)
+    pw[NP] = jnp.zeros((R, R), jnp.bfloat16)
     pltpu.make_async_copy(factors.at[pl.ds(0, T)], fac, fac_sem).wait()
     for x in range(T):
         fact[x] = fac[x].T
 
-    rowk = lax.broadcasted_iota(jnp.int32, (2 * BS, 256), 0) // BS
-    cols = lax.broadcasted_iota(jnp.int32, (2 * BS, 256), 1)
-    delta = cols - rowk
-
-    def halves(x, c):
+    eye = lax.broadcasted_iota(jnp.int32, (BS, BS), 0) == lax.broadcasted_iota(jnp.int32, (BS, BS), 1)
+
+    def halves(x, hs):
         pltpu.make_async_copy(recv.at[pl.ds(0, T)], dens.at[pl.ds(0, T)], in_sem.at[x]).wait()
         fx = fac[x]
         for yp in range(T // 2):
             s = x * T + 2 * yp
             d2 = jnp.concatenate([dens[s], dens[s + 1]], axis=1)
-            h2 = jnp.dot(fx, d2, preferred_element_type=jnp.float32).astype(jnp.bfloat16)
-            half[s] = h2[:, :BS]
-            half[s + 1] = h2[:, BS:]
-            f2 = jnp.concatenate([fac[2 * yp], fac[2 * yp + 1]], axis=1)
-            prod = (h2.astype(jnp.float32) * f2.astype(jnp.float32)).astype(jnp.bfloat16)
-            spread = (delta == s).astype(jnp.bfloat16)
-            pdt[...] += jnp.dot(prod, spread, preferred_element_type=jnp.float32)
+            hs[yp] = jnp.dot(fx, d2, preferred_element_type=jnp.float32).astype(jnp.bfloat16)
+
+    def pairs_of(x, hs):
+        for y in range(T):
+            s = x * T + y
+            h = hs[y // 2, :, (y % 2) * BS:(y % 2 + 1) * BS]
+            p = jnp.dot(h, fact[y], preferred_element_type=jnp.float32)
+            pw[s] = p.astype(jnp.bfloat16)
+            dia = [
+                jnp.sum(jnp.where(eye, p[k * BS:(k + 1) * BS, k * BS:(k + 1) * BS], 0.0), axis=0, keepdims=True)
+                for k in range(3)
+            ]
+            pot[s] = jnp.concatenate(dia, axis=1)
+
+    halves(0, ha)
+
+    def both(k, c):
+        halves(2 * k + 1, hb)
+        pairs_of(2 * k, ha)
+        halves(2 * k + 2, ha)
+        pairs_of(2 * k + 1, hb)
         return c
 
-    lax.fori_loop(0, T, halves, 0)
-    pair_diag = pdt[...].T
+    lax.fori_loop(0, T // 2 - 1, both, 0)
+    halves(T - 1, hb)
+    pairs_of(T - 2, ha)
+    pairs_of(T - 1, hb)
+    pair_diag = pot[...].reshape(NP, R)
     total = jnp.dot(coul[...], pair_diag, precision=lax.Precision.HIGHEST, preferred_element_type=jnp.float32)
     pot[...] = jnp.dot(total, core[...], precision=lax.Precision.HIGHEST, preferred_element_type=jnp.float32).reshape(NP, 1, R)
-    eye = lax.broadcasted_iota(jnp.int32, (BS, BS), 0) == lax.broadcasted_iota(jnp.int32, (BS, BS), 1)
-
-
-    def gather_pairs(lo, n, first, pairs):
-        hs, ws = [], []
-        for k in range(2 * pairs):
-            e = first + k
-            s = jnp.where(e < n, lst[lo + e], NP)
-            hs.append(half[s])
-            ws.append(fact[lax.rem(s, T)])
-        return jnp.dot(
-            jnp.concatenate(hs, axis=1), jnp.concatenate(ws, axis=0), preferred_element_type=jnp.float32
-        )
-
-    def with_diag(cm, row):
-        parts = []
-        for k in range(3):
-            line = cm[k * BS:(k + 1) * BS]
-            cols3 = [line[:, j * BS:(j + 1) * BS] for j in range(3)]
-            cols3[k] = cols3[k] + jnp.where(eye, row[:, k * BS:(k + 1) * BS], 0.0)
-            parts.append(jnp.concatenate(cols3, axis=1))
-        return jnp.concatenate(parts, axis=0).astype(jnp.bfloat16)
-
-    def step(i, c):
-        now = lax.rem(i, 2)
-        before = 1 - now
-        tg = [order[2 * G + i * G + q] for q in range(G)]
-        t1 = [order[G + i * G + q] for q in range(G)]
-        t2 = [order[i * G + q] for q in range(G)]
-
-        def exchange(t, q, pairs, extra):
-            lo = start[t]
-            n = start[t + 1] - lo
-            if extra:
-                acc[...] = jnp.zeros_like(acc)
-
-                def more(k, c):
-                    acc[...] += gather_pairs(lo, n, 2 * k, 1)
-                    return c
-
-                lax.fori_loop(pairs, (n + 1) // 2, more, 0)
-            if pairs:
-                es = gather_pairs(lo, n, 0, pairs)
+
+    def source(lo, n, e):
+        return jnp.where(e < n, tables[0, lo + e], NP)
+
+    def entry(lo, n, e, rows):
+        return pw[source(lo, n, e), rows].astype(jnp.float32)
+
+    def entries_at(lo, n, e, many, rows):
+        one = pw[source(lo, n, e), rows]
+        if many == 2:
+            one = one + pw[source(lo, n, e + 1), rows]
+        return one.astype(jnp.float32)
+
+    def put_core_matrices(ts, cms, count, extra, rows):
+        r = rows.start
+        block = r // BS
+        at = r % BS
+        weight = corem[rows]
+        mask = eye[at:at + STRIP]
+        for q, t in enumerate(ts):
+            lo = tables[1, t]
+            n = tables[1, t + 1] - lo
+            dia = jnp.where(mask, pot[t, :, block * BS:(block + 1) * BS], 0.0)
+            cols3 = [jnp.zeros((STRIP, BS), jnp.float32)] * 3
+            if count:
+                es = entries_at(lo, n, 0, min(2, count), rows)
+                for k in range(2, count, 2):
+                    es = es + entries_at(lo, n, k, min(2, count - k), rows)
                 if extra:
-                    es = es + acc[...]
-                cm = corem[...] * es
-            else:
-                cm = jnp.zeros((R, R), jnp.float32)
-            cms[now, q] = with_diag(cm, pot[t])
-
-        def late():
-            for q in range(G):
-                x2 = jnp.minimum(t2[q], NP - 1) // T
-                pieces[t2[q]] = jnp.dot(
-                    fact[x2], rhs[now, q], preferred_element_type=jnp.float32
-                ).astype(jnp.bfloat16)
-            for q in range(G):
-                y1 = lax.rem(t1[q], T)
-                rhs[before, q] = jnp.dot(
-                    cms[before, q], fac[y1], preferred_element_type=jnp.float32
-                ).astype(jnp.bfloat16)
-
-        def branch(pairs, extra):
+                    es = lax.fori_loop(count, n, lambda k, v: v + entry(lo, n, k, rows), es)
+                cm = weight * es
+                cols3 = [cm[:, j * BS:(j + 1) * BS] for j in range(3)]
+            cols3[block] = cols3[block] + dia
+            cms[q, rows] = jnp.concatenate(cols3, axis=1).astype(jnp.bfloat16)
+
+    def step(i, cm_now, cm_before, rh_now, rh_before):
+
+        def ranked(j):
+            return jnp.where(j >= 0, tables[2, jnp.maximum(j, 0)], NP)
+
+        tg = [ranked(i * G + q) for q in range(G)]
+        t1 = [ranked((i - 1) * G + q) for q in range(G)]
+        t2 = [ranked((i - 2) * G + q) for q in range(G)]
+
+        def late(q):
+            x2, _ = split(jnp.minimum(t2[q], NP - 1))
+            _, y1 = split(t1[q])
+            dens[t2[q]] = jnp.dot(fact[x2], rh_before[q], preferred_element_type=jnp.float32).astype(jnp.bfloat16)
+            rh_now[q] = jnp.dot(
+                cm_before[q], fac[y1], preferred_element_type=jnp.float32
+            ).astype(jnp.bfloat16)
+
+        def branch(count, extra):
             def run():
-                late()
-                for q in range(G):
-                    exchange(tg[q], q, pairs, extra)
+                strips = R // STRIP
+                for part in range(strips):
+                    for q in range(part * G // strips, (part + 1) * G // strips):
+                        late(q)
+                    if count is not None:
+                        put_core_matrices(tg, cm_now, count, extra, slice(part * STRIP, (part + 1) * STRIP))
             return run
 
-        top = start[tg[0] + 1] - start[tg[0]]
-        top = jnp.where(i < NP // G, (top + 1) // 2, -1)
+        top = tables[1, tg[0] + 1] - tables[1, tg[0]]
+        top = jnp.where(i < NP // G, top, -1)
         lax.switch(
             jnp.minimum(top, LEVELS + 1) + 1,
-            [late] + [branch(k, False) for k in range(LEVELS + 1)] + [branch(LEVELS, True)],
+            [branch(None, False)] + [branch(k, False) for k in range(LEVELS + 1)] + [branch(LEVELS, True)],
         )
-        for q in range(G):
-            @pl.when(i >= 2)
-            def _(q=q):
-                pltpu.make_async_copy(pieces.at[t2[q]], outbound.at[slot_of(direct, slots, t2[q])], out_sem).start()
+        @pl.when(i >= 2)
+        def _():
+            for q in range(G):
+                pltpu.make_async_copy(dens.at[t2[q]], outbound.at[slot_of(direct, slots, t2[q])], out_sem).start()
+
+    def steps(k, c):
+        step(2 * k, cma, cmb, rha, rhb)
+        step(2 * k + 1, cmb, cma, rhb, rha)
         return c
 
-    lax.fori_loop(0, NP // G + 2, step, 0)
-    pltpu.make_async_copy(pieces.at[pl.ds(0, NP)], outbound.at[pl.ds(0, NP)], out_sem).wait()
-
-
-def compute(ids, slots, lst, start, order, core, coul, recv, factors, nslots, direct=False):
+    lax.fori_loop(0, (NP // G + 2) // 2, steps, 0)
+    pltpu.make_async_copy(dens.at[pl.ds(0, NP)], outbound.at[pl.ds(0, NP)], out_sem).wait()
+
+
+def compute(ids, slots, tables, core, coul, recv, factors, nslots, direct=False):
     smem = pl.BlockSpec(memory_space=pltpu.SMEM)
     vmem = pl.BlockSpec(memory_space=pltpu.VMEM)
     hbm = pl.BlockSpec(memory_space=pl.ANY)
     return pl.pallas_call(
         functools.partial(compute_kernel, direct),
         out_shape=jax.ShapeDtypeStruct((nslots, BS, BS), jnp.bfloat16),
-        in_specs=[smem] * 5 + [vmem] * 2 + [hbm] * 2,
+        in_specs=[smem] * 3 + [vmem] * 2 + [hbm] * 2,
         out_specs=hbm,
         scratch_shapes=[
-            pltpu.VMEM((NP, BS, BS), jnp.bfloat16),
+            pltpu.VMEM((NP + 1, BS, BS), jnp.bfloat16),
             pltpu.VMEM((T, R, BS), jnp.bfloat16),
             pltpu.VMEM((T, BS, R), jnp.bfloat16),
-            pltpu.VMEM((NP + 1, R, BS), jnp.bfloat16),
-            pltpu.VMEM((NP + 1, BS, BS), jnp.bfloat16),
-            pltpu.VMEM((R, 256), jnp.float32),
+            pltpu.VMEM((NP + 1, R, R), jnp.bfloat16),
+            pltpu.VMEM((T // 2, R, 2 * BS), jnp.bfloat16),
+            pltpu.VMEM((T // 2, R, 2 * BS), jnp.bfloat16),
             pltpu.VMEM((R, R), jnp.float32),
             pltpu.VMEM((NP, 1, R), jnp.float32),
-            pltpu.VMEM((R, R), jnp.float32),
-            pltpu.VMEM((2, G, R, R), jnp.bfloat16),
-            pltpu.VMEM((2, G, R, BS), jnp.bfloat16),
+            pltpu.VMEM((G, R, R), jnp.bfloat16),
+            pltpu.VMEM((G, R, R), jnp.bfloat16),
+            pltpu.VMEM((G, R, BS), jnp.bfloat16),
+            pltpu.VMEM((G, R, BS), jnp.bfloat16),
             pltpu.SemaphoreType.DMA((T,)),
             pltpu.SemaphoreType.DMA,
             pltpu.SemaphoreType.DMA,
         ],
-        compiler_params=pltpu.CompilerParams(vmem_limit_bytes=50 * 2**20),
+        compiler_params=pltpu.CompilerParams(vmem_limit_bytes=59 * 2**20),
         cost_estimate=pl.CostEstimate(flops=25 * 10**9, bytes_accessed=12 * 10**6, transcendentals=0),
         name="fock_pieces_direct" if direct else "fock_pieces",
-    )(ids, slots, lst, start, order, core, coul, recv, factors)
-
-
-def coulomb_table(quads, count):
-    live = (jnp.arange(128, dtype=jnp.int32) < count).astype(jnp.float32)
-    p = quads[:, 0] * T + quads[:, 1]
-    q = quads[:, 2] * T + quads[:, 3]
-    tg = jnp.concatenate([p, q])
-    sr = jnp.concatenate([q, p])
-    ht = (tg[:, None] == jnp.arange(NP)[None]).astype(jnp.bfloat16)
-    hs = jnp.where(sr[:, None] == jnp.arange(256)[None], jnp.concatenate([live, live])[:, None] * 2.0, 0.0).astype(jnp.bfloat16)
-    return lax.dot_general(ht, hs, (((0,), (0,)), ((), ())), preferred_element_type=jnp.float32)
-
-
-CAP = 10
+    )(ids, slots, tables, core, coul, recv, factors)
+
+
+CAP = 9
 RELAY = 144
 MESH = pl.DeviceIdType.MESH
 ORDERS = ((2, 1, 0), (1, 0, 2), (0, 2, 1))
@@ -490,6 +461,59 @@
         copy.wait()
 
 
+def share_kernel(mine, density, ids, sibling, buf, line, send, recv, swap_send, swap_recv):
+    at = here()
+    x, y, z, c = at
+    barrier = pltpu.get_barrier_semaphore()
+    for axis in range(3):
+        for by in (1, 2, 3):
+            pl.semaphore_signal(barrier, inc=1, device_id=moved(at, axis, by), device_id_type=MESH)
+    pl.semaphore_signal(barrier, inc=1, device_id=device(x, y, z, 1 - c), device_id_type=MESH)
+    line[...] = jnp.zeros_like(line)
+    line[:, :T] = mine[...]
+    buf[z, y, x, c] = line[...]
+    pl.semaphore_wait(barrier, 10)
+    swap = pltpu.make_async_remote_copy(
+        density, sibling, swap_send, swap_recv, device_id=device(x, y, z, 1 - c), device_id_type=MESH
+    )
+    pair = pltpu.make_async_remote_copy(
+        buf.at[z, y, x, c], buf.at[z, y, x, c], send.at[9], recv.at[9],
+        device_id=device(x, y, z, 1 - c), device_id_type=MESH,
+    )
+    pair.start()
+    pair.wait()
+    swap.start()
+    for axis, held in ((0, buf.at[z, y, x]), (1, buf.at[z, y]), (2, buf.at[z])):
+        copies = [
+            pltpu.make_async_remote_copy(
+                held, held, send.at[3 * axis + by - 1], recv.at[3 * axis + by - 1],
+                device_id=moved(at, axis, by), device_id_type=MESH,
+            )
+            for by in (1, 2, 3)
+        ]
+        start_all(copies)
+        wait_all(copies)
+    for d in range(128):
+        ids[d:d + 1, :] = buf[d // 32, d // 8 % 4, d // 2 % 4, d % 2]
+    swap.wait()
+
+
+def share_tasks(mine, density):
+    vmem = pl.BlockSpec(memory_space=pltpu.VMEM)
+    hbm = pl.BlockSpec(memory_space=pl.ANY)
+    dma = pltpu.SemaphoreType.DMA
+    return pl.pallas_call(
+        share_kernel,
+        out_shape=[jax.ShapeDtypeStruct((128, 128), jnp.int32), jax.ShapeDtypeStruct((72, BS, BS), jnp.bfloat16)],
+        in_specs=[vmem, hbm],
+        out_specs=[vmem, hbm],
+        scratch_shapes=[pltpu.VMEM((4, 4, 4, 2, 1, 128), jnp.int32), pltpu.VMEM((1, 128), jnp.int32)]
+        + [dma((10,)), dma((10,)), dma, dma],
+        compiler_params=pltpu.CompilerParams(collective_id=3, has_side_effects=True),
+        name="share_tasks",
+    )(mine, density.reshape(72, BS, BS))
+
+
 def fetch_kernel(tab, lists, density, sibling, out, pool, r0, r1, r2, rs, a, b, d,
                  load, relay_send, relay_recv, send, recv, local):
     at = here()
@@ -526,7 +550,7 @@
         def fill(i, cc, k=k):
             index = tab[k, 2 * i + c]
             plain = pool[jnp.clip(index, 0, 143)]
-            passed = relayed[k][jnp.maximum(index - RELAY, 0)]
+            passed = relayed[k][jnp.clip(index - RELAY, 0, 2 * CAP - 1)]
             a[k, i // 16, i // 4 % 4, i % 4] = jnp.where(index >= RELAY, passed, plain)
             return cc
 
@@ -687,7 +711,7 @@
 
 def fast_path(density, factors, core, mine, sibling, tables, place, tab, lists, coul):
     recv = fetch_blocks(tab, lists, density, sibling).reshape(192, BS, BS)
-    pieces = compute(mine, tab[7], *tables, core, coul, recv, factors, 192)
+    pieces = compute(mine, tab[7], tables, core, coul, recv, factors, 192)
     got, back = return_pieces(lists, pieces.reshape(3, 4, 4, 4, BS, BS))
     own, other = collect(place, tab, lists, got, back)
     return (own + swap_cores(other).astype(jnp.float32)).reshape(24, 3, BS, BS)
@@ -794,29 +818,28 @@
     recv = lax.all_to_all(sent, axes, split_axis=0, concat_axis=0, tiled=True)
     owner = mine[:, None] // 24 * 32 + mine[None, :] // 3
     slot = (owner * 3 + (jnp.arange(T) % 3)[:, None]).reshape(-1)
-    pieces = compute(mine, mine, *tables, core, coul, recv[slot], factors, NP, direct=True)
+    pieces = compute(mine, mine, tables, core, coul, recv[slot], factors, NP, direct=True)
     outbound = jnp.zeros((384, BS, BS), jnp.bfloat16).at[slot].set(pieces)
     inbound = lax.all_to_all(outbound, axes, split_axis=0, concat_axis=0, tiled=True)
     return gather(where, ids, inbound)
 
 
 def shards(density, factors, core, task_blocks, quartets, quartet_count):
-    axes = ("row", "bulk")
     mine = task_blocks[0]
     bulk = lax.axis_index("bulk")
     place = jnp.stack([lax.axis_index("row"), bulk // 8, bulk // 2 % 4, bulk % 2]).astype(jnp.int32)
-    ids = lax.all_to_all(
-        jnp.broadcast_to(jnp.pad(mine, (0, 116))[None], (128, 128)), axes, split_axis=0, concat_axis=0, tiled=True
-    )
-    sibling = swap_cores(density)
-    tables = entries(quartets, quartet_count)
-    coul = coulomb_table(quartets, quartet_count[0])
+    ids, sibling = share_tasks(task_blocks, density)
+    tables, coul = entries(quartets, quartet_count)
     tab, lists = route(place, ids)
-    return lax.cond(
-        tab[7, 127] > 0,
-        lambda: slow_path(density, factors, core, mine, tables, place, ids, coul),
-        lambda: fast_path(density, factors, core, mine, sibling, tables, place, tab, lists, coul),
-    )
+    fock = fast_path(density, factors, core, mine, sibling, tables, place, tab, lists, coul)
+
+    def again(state):
+        return state[0]
+
+    def padded(state):
+        return jnp.array(False), slow_path(density, factors, core, mine, tables, place, ids, coul)
+
+    return lax.while_loop(again, padded, (tab[7, 127] > 0, fock))[1]
 
 
 def solution(mesh):

time: 358 us -> 305 us (0.85); the launches traced: 353 us -> 304 us
  Pallas kernels: 313 us -> 286 us
  starting transfers between devices: 12.7 us -> 0.95 us
  loops' own time: 10.1 us -> 0.01 us
    pallas_call x1, Pallas kernels: 71.4 us -> 56.9 us  [compute(): pl.pallas_call(functools.partial(compute_kernel, direct), out_shape=jax.S...]
    all_to_all x1 -> x0, starting transfers between devices: 10.2 us -> none  [shards(): lax.all_to_all(jnp.broadcast_to(jnp.pad(mine, (0, 116))[None], (128, 128)...]
    another operation x1, loops' own time: 10.1 us -> 0.01 us  [shards(): return lax.while_loop(again, padded, (tab[7, 127] > 0, fock))[1]]
    pallas_call x1, Pallas kernels: 104 us -> 94.4 us  [fetch_blocks(): pl.pallas_call(fetch_kernel, out_shape=jax.ShapeDtypeStruct((3, 4, 4, 4,...]
    pallas_call x1, Pallas kernels: 107 us -> 102 us  [return_pieces(): pl.pallas_call(return_kernel, out_shape=[jax.ShapeDtypeStruct((3, 4, 4, 4...]
    unnamed x1 -> x19, local copies, waits for them, and re-layouts: 0.79 us -> 4.48 us
    pallas_call x1 -> x2, Pallas kernels: 17.8 us -> 19.1 us  [the longest x1 17.2 us: share_tasks(): pl.pallas_call(share_kernel, out_shape=[jax.ShapeDtypeStruct((128, 128),...]
  transfers between devices with their start and end apart: 3 -> 1, of which waited for: 1 -> 1; matrix products, arithmetic and copies ran while one was open for 1% -> 0% of each run, Pallas kernels for 5% -> 0%
where the time goes in v3:
time: 305 us; the launch traced here: 304 us
  Pallas kernels  286 us (94%)
  other arithmetic  6.4 us (2%)
  local copies, waits for them, and re-layouts  6.35 us (2%)
  waiting for transfers between devices  3.08 us (1%)
    pallas_call x1, Pallas kernels, return_pieces(): pl.pallas_call(return_kernel, out_shape=[jax.ShapeDtypeStruct((3, 4, 4, 4...  102 us
    pallas_call x1, Pallas kernels, fetch_blocks(): pl.pallas_call(fetch_kernel, out_shape=jax.ShapeDtypeStruct((3, 4, 4, 4,...  94.4 us
    pallas_call x1, Pallas kernels, compute(): pl.pallas_call(functools.partial(compute_kernel, direct), out_shape=jax.S...  56.9 us
    pallas_call x1, Pallas kernels, share_tasks(): pl.pallas_call(share_kernel, out_shape=[jax.ShapeDtypeStruct((128, 128),...  17.2 us
    pallas_call x1, Pallas kernels, collect(): pl.pallas_call(collect_kernel, out_shape=[jax.ShapeDtypeStruct((72, BS, B...  11.8 us
  transfers between devices with their start and end apart: 1, of which 1 were waited for; matrix products, arithmetic and copies ran while one was open for 0% of the time, Pallas kernels for 0%

profile of v3, /device:TPU:1, one launch (start us, length us, event | category | flops | bytes accessed | tf_op | source)
XLA Modules:
  0.0 304.4 jit_solution(8996873951244982660)
XLA Ops:
  0.0 17.2 %share_tasks.1 = (s32[128,128]{1,0:T(8,128)S(1)}, bf16[72,128,128]{2,1,0:T(8,128)(2,1)}) custom-call(s32[1,12]{1,0:T(1,128)} %mine.1, bf16[72,128,128]{2,1,0:T(8,128)(2,1)} %bitcast.28), custom_call_target="tpu_custom_call" | custom-call | tf_op jit(solution)/shard_map/share_tasks/pallas_call | solution.py:505
  17.2 0.7 pad_add_fusion.1.place
  17.8 1.7 route_tasks.1
  19.5 1.2 slice_bitcast_fusion.slots
  20.8 1.4 copy.8.quads
  22.8 0.0 copy-start
  22.8 1.7 copy-done
  24.5 0.0 copy-start.2
  24.5 0.7 copy-done.2
  25.2 0.0 copy-start.5
  25.2 0.7 copy-done.5
  25.9 0.0 copy-start.9
  25.9 0.0 copy-start.10
  25.9 94.4 %fetch_blocks.1 = bf16[3,4,4,4,128,128]{5,4,3,2,1,0:T(8,128)(2,1)} custom-call(s32[8,128]{1,0:T(8,128)S(1)} %copy-done.5, s32[16,128]{1,0:T(8,128)S(1)} %copy-done.2, bf16[72,128,128]{2,1,0:T(8,128)(2,1)} %bitcast.29, bf16[72,128,128]{2,1,0:T(8,128)(2,1)S(1)} %copy-done), custom_call_target="tpu_custom_call" | custom-call | tf_op jit(solution)/shard_map/fetch_blocks/pallas_call | solution.py:576
  120.2 2.0 sort_entries.1
  122.2 0.0 copy-done.9
  122.2 0.0 copy-done.10
  122.2 0.0 copy-start.3
  122.2 56.9 %fock_pieces.1 = bf16[192,128,128]{2,1,0:T(8,128)(2,1)} custom-call(s32[12]{0:T(128)S(1)} %bitcast.37, s32[128]{0:T(128)} %slice_bitcast_fusion.slots, s32[8,640]{1,0:T(8,128)S(1)} %get-tuple-element.150.tables, f32[384,384]{1,0:T(8,128)S(1)} %copy-done.10, f32[144,144]{1,0:T(8,128)S(1)} %get-tuple-element.152.coul, bf16[192,128,128]{2,1,0:T(8,128)(2,1)} %bitcast.30, ...), custom_call_target="tpu_custom_call" | custom-call | flops 24999999488 | bytes 12000000 | tf_op jit(solution)/shard_map/fock_pieces/pallas_call | solution.py:239
  179.2 0.0 copy-start.6
  179.2 0.0 copy-start.7
  179.2 0.0 copy-done.3
  179.2 102.3 %return_pieces.1 = (bf16[3,4,4,4,128,128]{5,4,3,2,1,0:T(8,128)(2,1)}, bf16[3,18,128,128]{3,2,1,0:T(8,128)(2,1)S(1)}) custom-call(s32[16,128]{1,0:T(8,128)S(1)} %copy-done.3, bf16[3,4,4,4,128,128]{5,4,3,2,1,0:T(8,128)(2,1)} %bitcast.32), custom_call_target="tpu_custom_call" | custom-call | tf_op jit(solution)/shard_map/return_pieces/pallas_call | solution.py:641
  281.5 0.0 copy-done.6
  281.5 0.0 copy-done.7
  281.5 11.8 %collect_pieces.1 = (f32[72,128,128]{2,1,0:T(8,128)}, bf16[72,128,128]{2,1,0:T(8,128)(2,1)}) custom-call(s32[4]{0:T(128)S(1)} %copy-done.7, s32[8,128]{1,0:T(8,128)S(1)} %copy-done.6, s32[16,128]{1,0:T(8,128)S(1)} %copy-done.3, bf16[3,64,128,128]{3,2,1,0:T(8,128)(2,1)} %bitcast.31, bf16[3,18,128,128]{3,2,1,0:T(8,128)(2,1)S(1)} %get-tuple-element.92.back), custom_call_target="tpu_custom_call" | custom-call | tf_op jit(solution)/shard_map/collect_pieces/pallas_call | solution.py:694
  293.4 0.9 collective-permute-start
  294.3 0.6 slice.9
  295.6 3.1 %collective-permute-done = bf16[72,128,128]{2,1,0:T(8,128)(2,1)S(1)} collective-permute-done((bf16[72,128,128]{2,1,0:T(8,128)(2,1)}, bf16[72,128,128]{2,1,0:T(8,128)(2,1)S(1)}, u32[]{:S(2)}, u32[]{:S(2)}) %collective-permute-start) | collective-permute-done | bytes 2359328 | tf_op jit(solution)/shard_map/ppermute | solution.py:709
  298.7 0.0 copy-start.8
  298.7 5.7 %convert_add_fusion = f32[72,128,128]{2,1,0:T(8,128)} fusion(f32[72,128,128]{2,1,0:T(8,128)} %get-tuple-element.93, bf16[72,128,128]{2,1,0:T(8,128)(2,1)S(1)} %collective-permute-done), kind=kLoop, calls=%fused_computation.10 | loop fusion | flops 2359296 | bytes 11796480 | tf_op jit(solution)/shard_map/add | solution.py:717
  304.4 0.0 copy-done.8
  (1 shorter events, 0.0 us)
Async XLA Ops:
  22.8 1.7 copy-start
  24.5 0.7 copy-start.2
  25.2 0.7 copy-start.5
  25.9 96.3 %copy-start.9 = (s32[1,12]{1,0:T(1,128)S(1)}, s32[1,12]{1,0:T(1,128)}, u32[]{:S(2)}) copy-start(s32[1,12]{1,0:T(1,128)} %mine.1) | copy-start | bytes 148
  25.9 96.4 %copy-start.10 = (f32[384,384]{1,0:T(8,128)S(1)}, f32[384,384]{1,0:T(8,128)}, u32[]{:S(2)}) copy-start(f32[384,384]{1,0:T(8,128)} %core.1) | copy-start | bytes 1769476
  122.2 57.0 %copy-start.3 = (s32[16,128]{1,0:T(8,128)S(1)}, s32[16,128]{1,0:T(8,128)}, u32[]{:S(2)}) copy-start(s32[16,128]{1,0:T(8,128)} %get-tuple-element.87.lists) | copy-start | bytes 24580
  179.2 102.3 %copy-start.6 = (s32[8,128]{1,0:T(8,128)S(1)}, s32[8,128]{1,0:T(8,128)}, u32[]{:S(2)}) copy-start(s32[8,128]{1,0:T(8,128)} %get-tuple-element.86.tab) | copy-start | bytes 12292
  179.2 102.3 %copy-start.7 = (s32[4]{0:T(128)S(1)}, s32[4]{0:T(128)}, u32[]{:S(2)}) copy-start(s32[4]{0:T(128)} %pad_add_fusion.1.place) | copy-start | bytes 52
  293.4 5.3 %collective-permute-start = (bf16[72,128,128]{2,1,0:T(8,128)(2,1)}, bf16[72,128,128]{2,1,0:T(8,128)(2,1)S(1)}, u32[]{:S(2)}, u32[]{:S(2)}) collective-permute-start(bf16[72,128,128]{2,1,0:T(8,128)(2,1)} %get-tuple-element.94), channel_id=1, source_target_pairs={{0,1},{1,0},{2,3},{3,2},{4,5},{5,4},{6,7},{7,6},{8,9},{9,8},{10,11... | collective-permute-start | bytes 7077896 | tf_op jit(solution)/shard_map/ppermute | solution.py:709
  298.7 5.7 %copy-start.8 = (bf16[24,3,128,128]{3,2,1,0:T(8,128)(2,1)S(1)}, bf16[24,3,128,128]{3,2,1,0:T(8,128)(2,1)}, u32[]{:S(2)}) copy-start(bf16[24,3,128,128]{3,2,1,0:T(8,128)(2,1)} %param.8) | copy-start | bytes 7077892

commit v4 on v3

--- a/solution.py
+++ b/solution.py
@@ -20,7 +20,7 @@
 def entries_kernel(quads, count, tables, coul):
     f32 = jnp.float32
     live = lax.broadcasted_iota(jnp.int32, (128, 1), 0) < count[0]
-    q = quads[...]
+    q = jnp.concatenate([quads[...], jnp.zeros((4, 128), jnp.int32)], axis=0).astype(f32).T.astype(jnp.int32)
     a, b, c, e = (q[:, n:n + 1] for n in range(4))
     lanes = lax.broadcasted_iota(jnp.int32, (128, 256), 1)
 
@@ -81,7 +81,7 @@
         out_specs=[vmem, vmem],
         cost_estimate=pl.CostEstimate(flops=10000, bytes_accessed=10000, transcendentals=0),
         name="sort_entries",
-    )(quads, count)
+    )(quads.T, count)
 
 
 def split(t):
@@ -94,7 +94,7 @@
         return t
     x, y = split(t)
     z = (x * 11) >> 5
-    return (x - 3 * z) * 64 + z * 16 + ((y * 11) >> 5) * 4 + slots[y]
+    return (x - 3 * z) * 64 + z * 16 + ((y * 11) >> 5) * 4 + slots[7, y]
 
 
 def compute_kernel(direct, ids, slots, tables, core, coul, recv, factors, outbound,
@@ -286,7 +286,7 @@
     return chip, col, twice, over1, over2, where2, over_col, rel
 
 
-def route_kernel(place, ids, tab, lists, idt, plus_s, minus_s, rankp_s, rankm_s):
+def route_kernel(place, ids, tab, idt, plus_s, minus_s, rankp_s, rankm_s):
     z, y, x, c = place[0], place[1], place[2], place[3]
     idt[...] = ids[...].astype(jnp.float32).T.astype(jnp.int32)
     lane = lax.broadcasted_iota(jnp.int32, (1, 128), 1)
@@ -387,7 +387,7 @@
         out = jnp.where(l16 == 3 + k, listed(my_minus, my_rankm, value), out)
     out = jnp.where(l16 == 6, listed(from_left, rank_left, lane), out)
     out = jnp.where(l16 == 7, listed(from_right, rank_right, lane), out)
-    lists[...] = out
+    tab[8:24, :] = out
 
 
 def route(place, ids):
@@ -395,9 +395,9 @@
     vmem = pl.BlockSpec(memory_space=pltpu.VMEM)
     return pl.pallas_call(
         route_kernel,
-        out_shape=[jax.ShapeDtypeStruct((8, 128), jnp.int32), jax.ShapeDtypeStruct((16, 128), jnp.int32)],
+        out_shape=jax.ShapeDtypeStruct((24, 128), jnp.int32),
         in_specs=[smem, vmem],
-        out_specs=[vmem, vmem],
+        out_specs=vmem,
         scratch_shapes=[pltpu.VMEM((128, 128), jnp.int32)] + [pltpu.VMEM((32, 128), jnp.float32)] * 4,
         name="route_tasks",
     )(place, ids)
@@ -514,7 +514,7 @@
     )(mine, density.reshape(72, BS, BS))
 
 
-def fetch_kernel(tab, lists, density, sibling, out, pool, r0, r1, r2, rs, a, b, d,
+def fetch_kernel(tab, density, sibling, out, pool, r0, r1, r2, rs, a, b, d,
                  load, relay_send, relay_recv, send, recv, local):
     at = here()
     c = at[3]
@@ -529,8 +529,8 @@
     relays = []
     for k in range(3):
         def fill(j, cc, k=k):
-            rs[k, j] = pool[jnp.maximum(lists[j, k], 0)]
-            rs[k, CAP + j] = pool[jnp.maximum(lists[j, 3 + k], 0)]
+            rs[k, j] = pool[jnp.maximum(tab[8 + j, k], 0)]
+            rs[k, CAP + j] = pool[jnp.maximum(tab[8 + j, 3 + k], 0)]
             return cc
         lax.fori_loop(0, CAP, fill, 0)
         pair = [
@@ -568,7 +568,7 @@
         wait_all(steps[k])
 
 
-def fetch_blocks(tab, lists, density, sibling):
+def fetch_blocks(tab, density, sibling):
     smem = pl.BlockSpec(memory_space=pltpu.SMEM)
     hbm = pl.BlockSpec(memory_space=pl.ANY)
     cube = pltpu.VMEM((3, 4, 4, 4, BS, BS), jnp.bfloat16)
@@ -576,7 +576,7 @@
     return pl.pallas_call(
         fetch_kernel,
         out_shape=jax.ShapeDtypeStruct((3, 4, 4, 4, BS, BS), jnp.bfloat16),
-        in_specs=[smem, smem, hbm, hbm],
+        in_specs=[smem, hbm, hbm],
         out_specs=hbm,
         scratch_shapes=[pltpu.VMEM((144, BS, BS), jnp.bfloat16)]
         + [pltpu.VMEM((2 * CAP, BS, BS), jnp.bfloat16)] * 3
@@ -586,10 +586,10 @@
             collective_id=1, has_side_effects=True, vmem_limit_bytes=50 * 2**20
         ),
         name="fetch_blocks",
-    )(tab, lists, density.reshape(72, BS, BS), sibling.reshape(72, BS, BS))
-
-
-def return_kernel(lists, pieces, out, back, b, d, e0, e1, e2, rs,
+    )(tab, density.reshape(72, BS, BS), sibling.reshape(72, BS, BS))
+
+
+def return_kernel(tab, pieces, out, back, b, d, e0, e1, e2, rs,
                   relay_send, relay_recv, send, recv, local, store):
     at = here()
     greet(at)
@@ -614,7 +614,7 @@
 
         def fill(j, cc, k=k):
             for side in range(2):
-                t = jnp.maximum(lists[j, 6 + side], 0) // 2
+                t = jnp.maximum(tab[8 + j, 6 + side], 0) // 2
                 rs[k, side * CAP + j] = ends[k][t // 16, t // 4 % 4, t % 4]
             return cc
 
@@ -633,7 +633,7 @@
         wait_all(steps[k])
 
 
-def return_pieces(lists, pieces):
+def return_pieces(tab, pieces):
     smem = pl.BlockSpec(memory_space=pltpu.SMEM)
     hbm = pl.BlockSpec(memory_space=pl.ANY)
     cube = pltpu.VMEM((3, 4, 4, 4, BS, BS), jnp.bfloat16)
@@ -654,67 +654,84 @@
             collective_id=2, has_side_effects=True, vmem_limit_bytes=50 * 2**20
         ),
         name="return_pieces",
-    )(lists, pieces)
-
-
-def collect_kernel(place, tab, lists, got, back, own, other, acc):
+    )(tab, pieces)
+
+
+def collect_kernel(half, place, tab, got, back, *rest):
+    if half:
+        out, total, got_v, back_v, sems = rest
+    else:
+        part, out, got_v, back_v, sems = rest
+        total = out
     c = place[3]
-    acc[...] = jnp.zeros_like(acc)
-    own[...] = jnp.zeros_like(own)
+    loads = []
+    for k in range(3):
+        loads.append(
+            (
+                pltpu.make_async_copy(got.at[k], got_v.at[k], sems.at[0, k]),
+                pltpu.make_async_copy(back.at[k], back_v.at[k], sems.at[1, k]),
+            )
+        )
+        start_all(loads[k])
+    total[...] = jnp.zeros_like(total) if half else part[...].astype(jnp.float32)
 
     def put(index, block):
+        index = index - 72 * half
+
         @pl.when((index >= 0) & (index < 72))
         def _():
-            own[jnp.clip(index, 0, 71)] += block().astype(jnp.float32)
-
-        @pl.when((index >= 72) & (index < 144))
-        def _():
-            acc[jnp.clip(index - 72, 0, 71)] += block().astype(jnp.float32)
-
-    def add(i, cc):
-        for k in range(3):
-            put(tab[k, 2 * i + c], lambda: got[k, i])
-        return cc
-
-    lax.fori_loop(0, 64, add, 0)
-
-    def add_back(j, cc):
-        for k in range(3):
+            total[jnp.clip(index, 0, 71)] += block().astype(jnp.float32)
+
+    for k in range(3):
+        wait_all(loads[k])
+
+        def add(i, cc, k=k):
+            for n in range(4):
+                put(tab[k, 8 * i + 2 * n + c], lambda: got_v[k, 4 * i + n])
+            return cc
+
+        lax.fori_loop(0, 16, add, 0)
+
+        def add_back(j, cc, k=k):
             for side in range(2):
-                put(lists[j, 3 * side + k], lambda: back[k, side * CAP + j])
-        return cc
-
-    lax.fori_loop(0, CAP, add_back, 0)
-    other[...] = acc[...].astype(jnp.bfloat16)
-
-
-def collect(place, tab, lists, got, back):
+                put(tab[8 + j, 3 * side + k], lambda: back_v[k, side * CAP + j])
+            return cc
+
+        lax.fori_loop(0, CAP, add_back, 0)
+    if half:
+        out[...] = total[...].astype(jnp.bfloat16)
+
+
+def collect(half, place, tab, got, back, *part):
     smem = pl.BlockSpec(memory_space=pltpu.SMEM)
     vmem = pl.BlockSpec(memory_space=pltpu.VMEM)
+    hbm = pl.BlockSpec(memory_space=pl.ANY)
     return pl.pallas_call(
-        collect_kernel,
-        out_shape=[
-            jax.ShapeDtypeStruct((72, BS, BS), jnp.float32),
-            jax.ShapeDtypeStruct((72, BS, BS), jnp.bfloat16),
+        functools.partial(collect_kernel, half),
+        out_shape=jax.ShapeDtypeStruct((72, BS, BS), jnp.bfloat16 if half else jnp.float32),
+        in_specs=[smem, smem, hbm, hbm] + [vmem] * len(part),
+        out_specs=vmem,
+        scratch_shapes=([pltpu.VMEM((72, BS, BS), jnp.float32)] if half else [])
+        + [
+            pltpu.VMEM((3, 64, BS, BS), jnp.bfloat16),
+            pltpu.VMEM((3, 2 * CAP, BS, BS), jnp.bfloat16),
+            pltpu.SemaphoreType.DMA((2, 3)),
         ],
-        in_specs=[smem, smem, smem, vmem, vmem],
-        out_specs=[vmem, vmem],
-        scratch_shapes=[pltpu.VMEM((72, BS, BS), jnp.float32)],
         compiler_params=pltpu.CompilerParams(vmem_limit_bytes=50 * 2**20),
-        name="collect_pieces",
-    )(place, tab, lists, got.reshape(3, 64, BS, BS), back)
+        name="collect_sibling" if half else "collect_own",
+    )(place, tab, got.reshape(3, 64, BS, BS), back, *part)
 
 
 def swap_cores(value):
     return lax.ppermute(value, "bulk", [(i, i ^ 1) for i in range(32)])
 
 
-def fast_path(density, factors, core, mine, sibling, tables, place, tab, lists, coul):
-    recv = fetch_blocks(tab, lists, density, sibling).reshape(192, BS, BS)
-    pieces = compute(mine, tab[7], tables, core, coul, recv, factors, 192)
-    got, back = return_pieces(lists, pieces.reshape(3, 4, 4, 4, BS, BS))
-    own, other = collect(place, tab, lists, got, back)
-    return (own + swap_cores(other).astype(jnp.float32)).reshape(24, 3, BS, BS)
+def fast_path(density, factors, core, mine, sibling, tables, place, tab, coul):
+    recv = fetch_blocks(tab, density, sibling).reshape(192, BS, BS)
+    pieces = compute(mine, tab, tables, core, coul, recv, factors, 192)
+    got, back = return_pieces(tab, pieces.reshape(3, 4, 4, 4, BS, BS))
+    part = swap_cores(collect(1, place, tab, got, back))
+    return collect(0, place, tab, got, back, part).reshape(24, 3, BS, BS)
 
 
 def column_of(ids, d, bulk):
@@ -810,7 +827,7 @@
     )(place, ids, inbound)
 
 
-def slow_path(density, factors, core, mine, tables, place, ids, coul):
+def slow_path(density, factors, core, mine, tables, place, tab, ids, coul):
     axes = ("row", "bulk")
     where = jnp.stack([place[0], place[1] * 8 + place[2] * 2 + place[3]])
     ids = ids[:, :T].reshape(-1)
@@ -818,7 +835,7 @@
     recv = lax.all_to_all(sent, axes, split_axis=0, concat_axis=0, tiled=True)
     owner = mine[:, None] // 24 * 32 + mine[None, :] // 3
     slot = (owner * 3 + (jnp.arange(T) % 3)[:, None]).reshape(-1)
-    pieces = compute(mine, mine, tables, core, coul, recv[slot], factors, NP, direct=True)
+    pieces = compute(mine, tab, tables, core, coul, recv[slot], factors, NP, direct=True)
     outbound = jnp.zeros((384, BS, BS), jnp.bfloat16).at[slot].set(pieces)
     inbound = lax.all_to_all(outbound, axes, split_axis=0, concat_axis=0, tiled=True)
     return gather(where, ids, inbound)
@@ -830,14 +847,14 @@
     place = jnp.stack([lax.axis_index("row"), bulk // 8, bulk // 2 % 4, bulk % 2]).astype(jnp.int32)
     ids, sibling = share_tasks(task_blocks, density)
     tables, coul = entries(quartets, quartet_count)
-    tab, lists = route(place, ids)
-    fock = fast_path(density, factors, core, mine, sibling, tables, place, tab, lists, coul)
+    tab = route(place, ids)
+    fock = fast_path(density, factors, core, mine, sibling, tables, place, tab, coul)
 
     def again(state):
         return state[0]
 
     def padded(state):
-        return jnp.array(False), slow_path(density, factors, core, mine, tables, place, ids, coul)
+        return jnp.array(False), slow_path(density, factors, core, mine, tables, place, tab, ids, coul)
 
     return lax.while_loop(again, padded, (tab[7, 127] > 0, fock))[1]
 

time: 305 us -> 304 us (level)
  Pallas kernels: 286 us -> 293 us
  other arithmetic: 6.4 us -> 0.59 us
    add x1 -> x0, other arithmetic: 5.74 us -> none  [fast_path(): return (own + swap_cores(other).astype(jnp.float32)).reshape(24, 3, BS, BS)]
    pallas_call x2 -> x3, Pallas kernels: 13.5 us -> 18.3 us  [the longest x2 17.3 us: collect(): pl.pallas_call(functools.partial(collect_kernel, half), out_shape=jax.Sha...]
where the time goes in v4:
time: 304 us; the launch traced here: 303 us
  Pallas kernels  293 us (96%)
  local copies, waits for them, and re-layouts  3.7 us (1%)
  waiting for transfers between devices  3.23 us (1%)
    pallas_call x1, Pallas kernels, return_pieces(): pl.pallas_call(return_kernel, out_shape=[jax.ShapeDtypeStruct((3, 4, 4, 4...  104 us
    pallas_call x1, Pallas kernels, fetch_blocks(): pl.pallas_call(fetch_kernel, out_shape=jax.ShapeDtypeStruct((3, 4, 4, 4,...  94.4 us
    pallas_call x1, Pallas kernels, compute(): pl.pallas_call(functools.partial(compute_kernel, direct), out_shape=jax.S...  56.6 us
    pallas_call x2, Pallas kernels, collect(): pl.pallas_call(functools.partial(collect_kernel, half), out_shape=jax.Sha...  17.3 us
    pallas_call x1, Pallas kernels, share_tasks(): pl.pallas_call(share_kernel, out_shape=[jax.ShapeDtypeStruct((128, 128),...  17.2 us
  transfers between devices with their start and end apart: 1, of which 1 were waited for; matrix products, arithmetic and copies ran while one was open for 0% of the time, Pallas kernels for 0%

profile of v4, /device:TPU:1, one launch (start us, length us, event | category | flops | bytes accessed | tf_op | source)
XLA Modules:
  0.0 302.8 jit_solution(9432543815792119373)
XLA Ops:
  0.7 17.2 %share_tasks.1 = (s32[128,128]{1,0:T(8,128)S(1)}, bf16[72,128,128]{2,1,0:T(8,128)(2,1)}) custom-call(s32[1,12]{1,0:T(1,128)} %mine.1, bf16[72,128,128]{2,1,0:T(8,128)(2,1)} %bitcast.27), custom_call_target="tpu_custom_call" | custom-call | tf_op jit(solution)/shard_map/share_tasks/pallas_call | solution.py:505
  17.8 0.6 pad_add_fusion.1.place
  18.4 1.1 route_tasks.1.tab.slots
  19.5 0.0 copy-start
  19.5 1.7 copy-done
  21.2 0.0 copy-start.6
  21.2 0.0 copy-start.7
  21.2 94.4 %fetch_blocks.1 = bf16[3,4,4,4,128,128]{5,4,3,2,1,0:T(8,128)(2,1)} custom-call(s32[24,128]{1,0:T(8,128)S(1)} %route_tasks.1.tab.slots, bf16[72,128,128]{2,1,0:T(8,128)(2,1)} %bitcast.28, bf16[72,128,128]{2,1,0:T(8,128)(2,1)S(1)} %copy-done), custom_call_target="tpu_custom_call" | custom-call | tf_op jit(solution)/shard_map/fetch_blocks/pallas_call | solution.py:576
  115.6 1.8 sort_entries.1
  117.4 0.0 copy-done.6
  117.4 0.0 copy-done.7
  117.4 56.6 %fock_pieces.1 = bf16[192,128,128]{2,1,0:T(8,128)(2,1)} custom-call(s32[12]{0:T(128)S(1)} %bitcast.38, s32[24,128]{1,0:T(8,128)S(1)} %route_tasks.1.tab.slots, s32[8,640]{1,0:T(8,128)S(1)} %get-tuple-element.151.tables, f32[384,384]{1,0:T(8,128)S(1)} %copy-done.7, f32[144,144]{1,0:T(8,128)S(1)} %get-tuple-element.153.coul, bf16[192,128,128]{2,1,0:T(8,128)(2,1)} %bitcast.31, ...), custom_call_target="tpu_custom_call" | custom-call | flops 24999999488 | bytes 12000000 | tf_op jit(solution)/shard_map/fock_pieces/pallas_call | solution.py:239
  174.0 0.0 copy-start.3
  174.1 104.3 %return_pieces.1 = (bf16[3,4,4,4,128,128]{5,4,3,2,1,0:T(8,128)(2,1)}, bf16[3,18,128,128]{3,2,1,0:T(8,128)(2,1)S(1)}) custom-call(s32[24,128]{1,0:T(8,128)S(1)} %route_tasks.1.tab.slots, bf16[3,4,4,4,128,128]{5,4,3,2,1,0:T(8,128)(2,1)} %bitcast.32), custom_call_target="tpu_custom_call" | custom-call | tf_op jit(solution)/shard_map/return_pieces/pallas_call | solution.py:641
  278.4 0.0 copy-done.3
  278.4 8.0 %collect_sibling.1 = bf16[72,128,128]{2,1,0:T(8,128)(2,1)} custom-call(s32[4]{0:T(128)S(1)} %copy-done.3, s32[24,128]{1,0:T(8,128)S(1)} %route_tasks.1.tab.slots, bf16[3,64,128,128]{3,2,1,0:T(8,128)(2,1)} %bitcast.29, bf16[3,18,128,128]{3,2,1,0:T(8,128)(2,1)S(1)} %get-tuple-element.91.back), custom_call_target="tpu_custom_call" | custom-call | tf_op jit(solution)/shard_map/collect_sibling/pallas_call | solution.py:709
  286.4 1.0 collective-permute-start
  287.3 0.6 slice.9
  288.5 0.0 copy-start.4
  288.5 3.2 %collective-permute-done.rest_0_ = bf16[72,128,128]{2,1,0:T(8,128)(2,1)S(1)} collective-permute-done((bf16[72,128,128]{2,1,0:T(8,128)(2,1)}, bf16[72,128,128]{2,1,0:T(8,128)(2,1)S(1)}, u32[]{:S(2)}, u32[]{:S(2)}) %collective-permute-start) | collective-permute-done | bytes 2359328 | tf_op jit(solution)/shard_map/ppermute | solution.py:726
  291.7 0.0 copy-start.5
  291.7 1.5 copy-done.5
  293.2 9.3 %collect_own.1 = f32[72,128,128]{2,1,0:T(8,128)} custom-call(s32[4]{0:T(128)S(1)} %copy-done.3, s32[24,128]{1,0:T(8,128)S(1)} %route_tasks.1.tab.slots, bf16[3,64,128,128]{3,2,1,0:T(8,128)(2,1)} %bitcast.30, bf16[3,18,128,128]{3,2,1,0:T(8,128)(2,1)S(1)} %get-tuple-element.91.back, bf16[72,128,128]{2,1,0:T(8,128)(2,1)} %copy-done.5), custom_call_target="tpu_custom_call" | custom-call | tf_op jit(solution)/shard_map/collect_own/pallas_call | solution.py:709
  302.5 0.0 copy-done.4
  302.5 0.1 while.9
Async XLA Ops:
  19.5 1.7 copy-start
  21.2 96.2 %copy-start.6 = (s32[1,12]{1,0:T(1,128)S(1)}, s32[1,12]{1,0:T(1,128)}, u32[]{:S(2)}) copy-start(s32[1,12]{1,0:T(1,128)} %mine.1) | copy-start | bytes 148
  21.2 96.2 %copy-start.7 = (f32[384,384]{1,0:T(8,128)S(1)}, f32[384,384]{1,0:T(8,128)}, u32[]{:S(2)}) copy-start(f32[384,384]{1,0:T(8,128)} %core.1) | copy-start | bytes 1769476
  174.0 104.3 %copy-start.3 = (s32[4]{0:T(128)S(1)}, s32[4]{0:T(128)}, u32[]{:S(2)}) copy-start(s32[4]{0:T(128)} %pad_add_fusion.1.place) | copy-start | bytes 52
  286.4 5.4 %collective-permute-start = (bf16[72,128,128]{2,1,0:T(8,128)(2,1)}, bf16[72,128,128]{2,1,0:T(8,128)(2,1)S(1)}, u32[]{:S(2)}, u32[]{:S(2)}) collective-permute-start(bf16[72,128,128]{2,1,0:T(8,128)(2,1)} %collect_sibling.1), channel_id=1, source_target_pairs={{0,1},{1,0},{2,3},{3,2},{4,5},{5,4},{6,7},{7,6},{8,9},{9,8},{10,11... | collective-permute-start | bytes 7077896 | tf_op jit(solution)/shard_map/ppermute | solution.py:726
  288.5 14.0 %copy-start.4 = (bf16[24,3,128,128]{3,2,1,0:T(8,128)(2,1)S(1)}, bf16[24,3,128,128]{3,2,1,0:T(8,128)(2,1)}, u32[]{:S(2)}) copy-start(bf16[24,3,128,128]{3,2,1,0:T(8,128)(2,1)} %param.8) | copy-start | bytes 7077892
  291.7 1.5 copy-start.5

commit v5 on v4

--- a/solution.py
+++ b/solution.py
@@ -471,19 +471,13 @@
     pl.semaphore_signal(barrier, inc=1, device_id=device(x, y, z, 1 - c), device_id_type=MESH)
     line[...] = jnp.zeros_like(line)
     line[:, :T] = mine[...]
-    buf[z, y, x, c] = line[...]
+    buf[c, z, y, x] = line[...]
     pl.semaphore_wait(barrier, 10)
     swap = pltpu.make_async_remote_copy(
         density, sibling, swap_send, swap_recv, device_id=device(x, y, z, 1 - c), device_id_type=MESH
     )
-    pair = pltpu.make_async_remote_copy(
-        buf.at[z, y, x, c], buf.at[z, y, x, c], send.at[9], recv.at[9],
-        device_id=device(x, y, z, 1 - c), device_id_type=MESH,
-    )
-    pair.start()
-    pair.wait()
     swap.start()
-    for axis, held in ((0, buf.at[z, y, x]), (1, buf.at[z, y]), (2, buf.at[z])):
+    for axis, held in ((0, buf.at[c, z, y, x]), (1, buf.at[c, z, y]), (2, buf.at[c, z])):
         copies = [
             pltpu.make_async_remote_copy(
                 held, held, send.at[3 * axis + by - 1], recv.at[3 * axis + by - 1],
@@ -493,8 +487,14 @@
         ]
         start_all(copies)
         wait_all(copies)
+    pair = pltpu.make_async_remote_copy(
+        buf.at[c], buf.at[c], send.at[9], recv.at[9],
+        device_id=device(x, y, z, 1 - c), device_id_type=MESH,
+    )
+    pair.start()
+    pair.wait()
     for d in range(128):
-        ids[d:d + 1, :] = buf[d // 32, d // 8 % 4, d // 2 % 4, d % 2]
+        ids[d:d + 1, :] = buf[d % 2, d // 32, d // 8 % 4, d // 2 % 4]
     swap.wait()
 
 
@@ -507,7 +507,7 @@
         out_shape=[jax.ShapeDtypeStruct((128, 128), jnp.int32), jax.ShapeDtypeStruct((72, BS, BS), jnp.bfloat16)],
         in_specs=[vmem, hbm],
         out_specs=[vmem, hbm],
-        scratch_shapes=[pltpu.VMEM((4, 4, 4, 2, 1, 128), jnp.int32), pltpu.VMEM((1, 128), jnp.int32)]
+        scratch_shapes=[pltpu.VMEM((2, 4, 4, 4, 1, 128), jnp.int32), pltpu.VMEM((1, 128), jnp.int32)]
         + [dma((10,)), dma((10,)), dma, dma],
         compiler_params=pltpu.CompilerParams(collective_id=3, has_side_effects=True),
         name="share_tasks",

time: 304 us -> 309 us (1.016)
  Pallas kernels: 293 us -> 299 us
    pallas_call x1, Pallas kernels: 56.6 us -> 60.8 us  [compute(): pl.pallas_call(functools.partial(compute_kernel, direct), out_shape=jax.S...]
where the time goes in v5:
time: 309 us
  Pallas kernels  299 us (97%)
  local copies, waits for them, and re-layouts  3.7 us (1%)
  waiting for transfers between devices  3.23 us (1%)
    pallas_call x1, Pallas kernels, return_pieces(): pl.pallas_call(return_kernel, out_shape=[jax.ShapeDtypeStruct((3, 4, 4, 4...  103 us
    pallas_call x1, Pallas kernels, fetch_blocks(): pl.pallas_call(fetch_kernel, out_shape=jax.ShapeDtypeStruct((3, 4, 4, 4,...  95.8 us
    pallas_call x1, Pallas kernels, compute(): pl.pallas_call(functools.partial(compute_kernel, direct), out_shape=jax.S...  60.8 us
    pallas_call x1, Pallas kernels, share_tasks(): pl.pallas_call(share_kernel, out_shape=[jax.ShapeDtypeStruct((128, 128),...  19.6 us
    pallas_call x2, Pallas kernels, collect(): pl.pallas_call(functools.partial(collect_kernel, half), out_shape=jax.Sha...  17.1 us
  transfers between devices with their start and end apart: 1, of which 1 were waited for; matrix products, arithmetic and copies ran while one was open for 0% of the time, Pallas kernels for 0%

profile of v5, /device:TPU:1, one launch (start us, length us, event | category | flops | bytes accessed | tf_op | source)
XLA Modules:
  0.0 309.2 jit_solution(380571428087949671)
XLA Ops:
  0.7 19.6 %share_tasks.1 = (s32[128,128]{1,0:T(8,128)S(1)}, bf16[72,128,128]{2,1,0:T(8,128)(2,1)}) custom-call(s32[1,12]{1,0:T(1,128)} %mine.1, bf16[72,128,128]{2,1,0:T(8,128)(2,1)} %bitcast.27), custom_call_target="tpu_custom_call" | custom-call | tf_op jit(solution)/shard_map/share_tasks/pallas_call | solution.py:505
  20.3 0.6 pad_add_fusion.1.place
  20.9 1.1 route_tasks.1.tab.slots
  22.0 0.0 copy-start
  22.0 1.7 copy-done
  23.7 0.0 copy-start.6
  23.7 0.0 copy-start.7
  23.7 95.8 %fetch_blocks.1 = bf16[3,4,4,4,128,128]{5,4,3,2,1,0:T(8,128)(2,1)} custom-call(s32[24,128]{1,0:T(8,128)S(1)} %route_tasks.1.tab.slots, bf16[72,128,128]{2,1,0:T(8,128)(2,1)} %bitcast.28, bf16[72,128,128]{2,1,0:T(8,128)(2,1)S(1)} %copy-done), custom_call_target="tpu_custom_call" | custom-call | tf_op jit(solution)/shard_map/fetch_blocks/pallas_call | solution.py:576
  119.4 1.8 sort_entries.1
  121.3 0.0 copy-done.6
  121.3 0.0 copy-done.7
  121.3 60.8 %fock_pieces.1 = bf16[192,128,128]{2,1,0:T(8,128)(2,1)} custom-call(s32[12]{0:T(128)S(1)} %bitcast.38, s32[24,128]{1,0:T(8,128)S(1)} %route_tasks.1.tab.slots, s32[8,640]{1,0:T(8,128)S(1)} %get-tuple-element.151.tables, f32[384,384]{1,0:T(8,128)S(1)} %copy-done.7, f32[144,144]{1,0:T(8,128)S(1)} %get-tuple-element.153.coul, bf16[192,128,128]{2,1,0:T(8,128)(2,1)} %bitcast.31, ...), custom_call_target="tpu_custom_call" | custom-call | flops 24999999488 | bytes 12000000 | tf_op jit(solution)/shard_map/fock_pieces/pallas_call | solution.py:239
  182.1 0.0 copy-start.3
  182.1 102.8 %return_pieces.1 = (bf16[3,4,4,4,128,128]{5,4,3,2,1,0:T(8,128)(2,1)}, bf16[3,18,128,128]{3,2,1,0:T(8,128)(2,1)S(1)}) custom-call(s32[24,128]{1,0:T(8,128)S(1)} %route_tasks.1.tab.slots, bf16[3,4,4,4,128,128]{5,4,3,2,1,0:T(8,128)(2,1)} %bitcast.32), custom_call_target="tpu_custom_call" | custom-call | tf_op jit(solution)/shard_map/return_pieces/pallas_call | solution.py:641
  285.0 0.0 copy-done.3
  285.0 7.9 %collect_sibling.1 = bf16[72,128,128]{2,1,0:T(8,128)(2,1)} custom-call(s32[4]{0:T(128)S(1)} %copy-done.3, s32[24,128]{1,0:T(8,128)S(1)} %route_tasks.1.tab.slots, bf16[3,64,128,128]{3,2,1,0:T(8,128)(2,1)} %bitcast.29, bf16[3,18,128,128]{3,2,1,0:T(8,128)(2,1)S(1)} %get-tuple-element.91.back), custom_call_target="tpu_custom_call" | custom-call | tf_op jit(solution)/shard_map/collect_sibling/pallas_call | solution.py:709
  292.9 1.0 collective-permute-start
  293.9 0.6 slice.9
  295.0 0.0 copy-start.4
  295.0 3.2 %collective-permute-done.rest_0_ = bf16[72,128,128]{2,1,0:T(8,128)(2,1)S(1)} collective-permute-done((bf16[72,128,128]{2,1,0:T(8,128)(2,1)}, bf16[72,128,128]{2,1,0:T(8,128)(2,1)S(1)}, u32[]{:S(2)}, u32[]{:S(2)}) %collective-permute-start) | collective-permute-done | bytes 2359328 | tf_op jit(solution)/shard_map/ppermute | solution.py:726
  298.3 0.0 copy-start.5
  298.3 1.5 copy-done.5
  299.7 9.2 %collect_own.1 = f32[72,128,128]{2,1,0:T(8,128)} custom-call(s32[4]{0:T(128)S(1)} %copy-done.3, s32[24,128]{1,0:T(8,128)S(1)} %route_tasks.1.tab.slots, bf16[3,64,128,128]{3,2,1,0:T(8,128)(2,1)} %bitcast.30, bf16[3,18,128,128]{3,2,1,0:T(8,128)(2,1)S(1)} %get-tuple-element.91.back, bf16[72,128,128]{2,1,0:T(8,128)(2,1)} %copy-done.5), custom_call_target="tpu_custom_call" | custom-call | tf_op jit(solution)/shard_map/collect_own/pallas_call | solution.py:709
  308.9 0.0 copy-done.4
  308.9 0.1 while.9
Async XLA Ops:
  22.0 1.7 copy-start
  23.7 97.6 %copy-start.6 = (s32[1,12]{1,0:T(1,128)S(1)}, s32[1,12]{1,0:T(1,128)}, u32[]{:S(2)}) copy-start(s32[1,12]{1,0:T(1,128)} %mine.1) | copy-start | bytes 148
  23.7 97.6 %copy-start.7 = (f32[384,384]{1,0:T(8,128)S(1)}, f32[384,384]{1,0:T(8,128)}, u32[]{:S(2)}) copy-start(f32[384,384]{1,0:T(8,128)} %core.1) | copy-start | bytes 1769476
  182.1 102.9 %copy-start.3 = (s32[4]{0:T(128)S(1)}, s32[4]{0:T(128)}, u32[]{:S(2)}) copy-start(s32[4]{0:T(128)} %pad_add_fusion.1.place) | copy-start | bytes 52
  292.9 5.4 %collective-permute-start = (bf16[72,128,128]{2,1,0:T(8,128)(2,1)}, bf16[72,128,128]{2,1,0:T(8,128)(2,1)S(1)}, u32[]{:S(2)}, u32[]{:S(2)}) collective-permute-start(bf16[72,128,128]{2,1,0:T(8,128)(2,1)} %collect_sibling.1), channel_id=1, source_target_pairs={{0,1},{1,0},{2,3},{3,2},{4,5},{5,4},{6,7},{7,6},{8,9},{9,8},{10,11... | collective-permute-start | bytes 7077896 | tf_op jit(solution)/shard_map/ppermute | solution.py:726
  295.0 13.9 %copy-start.4 = (bf16[24,3,128,128]{3,2,1,0:T(8,128)(2,1)S(1)}, bf16[24,3,128,128]{3,2,1,0:T(8,128)(2,1)}, u32[]{:S(2)}) copy-start(bf16[24,3,128,128]{3,2,1,0:T(8,128)(2,1)} %param.8) | copy-start | bytes 7077892
  298.3 1.5 copy-start.5
